TPU v7x, 256 devices: a whole 4x4x8 slice. The times are simulated.
256 devices in a mesh: grp: 16 (over x_hi, z), blk: 16 (over x_lo, y, core).
Axes of the slice: x: 4 (x_hi: 2, x_lo: 2; x = x_hi * 2 + x_lo), y: 4, z: 8, core: 2. Of those that a mesh axis runs over, the one named last changes fastest.
Arguments:
- prompt_of: int32 [2048], P(('grp', 'blk')), may hold values from 0 to 31, as said below
- suffix_len: int32 [2048], P(('grp', 'blk')), may hold values from 1 to 256, as said below
- query: bfloat16 [2048, 4096], P(('grp', 'blk')), may hold values from -8 to 23
- new_key: bfloat16 [2048, 512], P(('grp', 'blk')), may hold values from -5 to 6
- new_value: bfloat16 [2048, 512], P(('grp', 'blk')), may hold values from -6 to 6
- suffix_key: bfloat16 [2048, 256, 512], P(('grp', 'blk')), may hold values from -5 to 6
- suffix_value: bfloat16 [2048, 256, 512], P(('grp', 'blk')), may hold values from -6 to 6
- prefix_key: bfloat16 [32, 4096, 512], P('grp', 'blk'), may hold values from -5 to 6
- prefix_value: bfloat16 [32, 4096, 512], P('grp', 'blk'), may hold values from -6 to 6
Outputs:
- attended: bfloat16 [2048, 4096], P(('grp', 'blk'))
Inputs may be any that keep to these rules, and one draw needn't show every extreme that they name: `prompt_of`: on every device at most 2 of its completions name prompts of one group (the group of a prompt is prompt // 2); one group gets exactly 2 from every device. `suffix_len`: some completion has exactly 256 cached suffix tokens.
All inputs are finite; a program needn't handle non-finite values.
Results may differ from a plain program's by a relative error of at most 0.0037.
Values may be sent and summed in bfloat16 or wider, within the bound.
No kernel may reach another device: no remote copies, remote signals or barrier semaphores. Data moves between devices by JAX's collectives and lax.ppermute only.
A program may use at most 128 MiB of HBM per device.

v0:
```python
import math

import jax
import jax.numpy as jnp
from jax import lax
from jax.experimental import pallas as pl
from jax.experimental.pallas import tpu as pltpu
from jax.sharding import Mesh, PartitionSpec as P

HD = 128
CAP = 2
HELD = 8
HEADS = 32
KVH = 4
RATIO = 8
PROMPTS = 32
SUF = 256
PIECE = 256
SLOTS = 256
ROWS = SLOTS * RATIO
NEG = -1e30
SCALE = HD ** (-0.5)
LOG2E = 1.4426950408889634
ALL = ("xh", "z", "xl", "y", "c")
NEAR = ("xl", "y")
FAR = ("xh", "z", "xl")


def slots_of(prompt_ref):
    prompts = [prompt_ref[i] for i in range(HELD)]
    slots = []
    for i in range(HELD):
        rank = jnp.int32(0)
        for j in range(i):
            rank = rank + jnp.where(prompts[j] == prompts[i], 1, 0)
        slots.append(prompts[i] * CAP + rank)
    return slots


def spread(values, index):
    picked = jnp.zeros(index.shape, jnp.int32)
    for i, value in enumerate(values):
        picked = jnp.where(index == i, value, picked)
    return picked


def prep_kernel(place_ref, prompt_hbm, query_hbm, key_ref, value_ref, send_ref, *refs):
    cut_refs = refs[:8]
    prompt_ref, query_ref, small_sem, cut_sem = refs[8:]
    small = [
        pltpu.make_async_copy(prompt_hbm, prompt_ref, small_sem.at[0]),
        pltpu.make_async_copy(query_hbm, query_ref, small_sem.at[1]),
    ]
    for copy in small:
        copy.start()
    place = place_ref[0]
    copies = []
    for step, cut_ref in enumerate(cut_refs):
        target = place ^ step
        prompt = target >> 2
        column = pl.multiple_of((target & 3) * HD, HD)
        for n, cache in enumerate((key_ref, value_ref)):
            copies.append(
                pltpu.make_async_copy(
                    cache.at[prompt, :, pl.ds(column, HD)], cut_ref.at[n], cut_sem.at[step, n]
                )
            )
            copies[-1].start()
    for copy in small:
        copy.wait()
    slots = slots_of(prompt_ref)
    lane = lax.broadcasted_iota(jnp.int32, (HELD, HD), 1)
    row = lax.broadcasted_iota(jnp.int32, (HELD, HD), 0)
    tags = jnp.concatenate(
        [spread(slots, lane & 7).astype(jnp.float32), spread(slots, row).astype(jnp.float32)], axis=0
    ).astype(jnp.bfloat16)
    for y in range(KVH):
        send_ref[y, :64] = jnp.concatenate(
            [
                query_ref[:, h * HD : (h + 1) * HD].astype(jnp.float32)
                for h in range(y * RATIO, (y + 1) * RATIO)
            ],
            axis=0,
        ).astype(jnp.bfloat16)
        send_ref[y, 64:] = tags
    for copy in copies:
        copy.wait()


def pack_kernel(got_ref, *refs):
    out_ref = refs[-1]
    held = got_ref[:, :64].reshape(256, HD)
    tags = [got_ref[y, 64:].astype(jnp.float32)[:1].astype(jnp.int32) for y in range(KVH)]
    half = lax.broadcasted_iota(jnp.int32, (1, HD), 1) < 64
    tag = jnp.concatenate([jnp.where(half, tags[0], tags[1]), jnp.where(half, tags[2], tags[3])], axis=1)
    lane_key = (lax.broadcasted_iota(jnp.int32, (1, 256), 1) >> 3) * 64 + tag
    chunk = 512
    for start in range(0, ROWS, chunk):
        row = lax.broadcasted_iota(jnp.int32, (chunk, 1), 0) + start
        row_key = ((row >> 1) & 3) * 512 + ((row >> 3) & 7) * 64 + (row >> 6) * 2 + (row & 1)
        select = (row_key == lane_key).astype(jnp.float32).astype(jnp.bfloat16)
        out_ref[start : start + chunk, :] = jnp.dot(
            select, held, preferred_element_type=jnp.float32
        ).astype(jnp.bfloat16)


def near_kernel(
    len_ref, query_ref, new_key_ref, new_value_ref, key_ref, value_ref, out_ref, heads_ref
):
    step = pl.program_id(0)

    @pl.when(step == 0)
    def _():
        for h in range(HEADS):
            heads_ref[h] = query_ref[:, h * HD : (h + 1) * HD].astype(jnp.float32)

    length = len_ref[step]
    query = heads_ref[:, pl.ds(step, 1), :].reshape(HEADS, HD)
    keys = key_ref[0]
    values = value_ref[0]
    held_row = lax.broadcasted_iota(jnp.int32, (HELD, 1), 0)

    def row_of(ref):
        rows = jnp.where(held_row == step, ref[...].astype(jnp.float32), 0.0)
        return jnp.sum(rows, axis=0, keepdims=True)

    new_key = row_of(new_key_ref)
    new_value = row_of(new_value_ref)

    def spread_heads(row):
        return jnp.concatenate(
            [jnp.broadcast_to(row[:, k * HD : (k + 1) * HD], (RATIO, HD)) for k in range(KVH)], axis=0
        )

    scores = jnp.concatenate(
        [
            lax.dot_general(
                query.astype(jnp.bfloat16),
                keys[:, k * HD : (k + 1) * HD],
                (((1,), (1,)), ((), ())),
                preferred_element_type=jnp.float32,
            )[k * RATIO : (k + 1) * RATIO]
            for k in range(KVH)
        ],
        axis=0,
    ) * SCALE
    own = jnp.sum(query * spread_heads(new_key), axis=1, keepdims=True) * SCALE
    live = lax.broadcasted_iota(jnp.int32, (1, SUF), 1) < length
    scores = jnp.where(live, scores, NEG)
    top = jnp.maximum(jnp.max(scores, axis=1, keepdims=True), own)
    weights = jnp.where(live, jnp.exp(scores - top), 0.0)
    own_weight = jnp.exp(own - top)
    total = jnp.sum(weights, axis=1, keepdims=True) + own_weight
    rounded = weights.astype(jnp.bfloat16)
    mixed = jnp.concatenate(
        [
            jnp.dot(rounded, values[:, k * HD : (k + 1) * HD], preferred_element_type=jnp.float32)[
                k * RATIO : (k + 1) * RATIO
            ]
            for k in range(KVH)
        ],
        axis=0,
    )
    mixed = mixed + own_weight.astype(jnp.bfloat16).astype(jnp.float32) * spread_heads(new_value)
    out_ref[:HEADS, pl.ds(step, 1), :] = (mixed / total).reshape(HEADS, 1, HD)
    out_ref[HEADS:, pl.ds(step, 1), :] = jnp.broadcast_to(top + jnp.log(total), (HEADS, HD)).reshape(
        HEADS, 1, HD
    )


def far_kernel(query_ref, *refs):
    pieces = refs[:16]
    out_ref, score_ref, query_scr, mixed_scr, stat_scr = refs[16:]
    span = 32
    block = span * RATIO
    tokens = 16 * PIECE
    queries = query_ref[...].astype(jnp.float32).reshape(32, RATIO, 8, HD)
    biggest = jnp.max(jnp.max(jnp.abs(queries), axis=1).reshape(SLOTS, HD), axis=1, keepdims=True)
    valid = (biggest > 0).astype(jnp.float32)
    row = lax.broadcasted_iota(jnp.int32, (SLOTS, SLOTS), 0)
    lane = lax.broadcasted_iota(jnp.int32, (SLOTS, SLOTS), 1)
    wide = jnp.broadcast_to(valid, (SLOTS, SLOTS)).astype(jnp.bfloat16)
    before = jnp.dot(
        (lane < row).astype(jnp.float32).astype(jnp.bfloat16), wide, preferred_element_type=jnp.float32
    )
    order = jnp.where(valid > 0, before, -1.0).astype(jnp.int32)
    gather = (order == lane).astype(jnp.float32).astype(jnp.bfloat16)
    count = jnp.sum(valid).astype(jnp.int32)
    for h in range(RATIO):
        query_scr[h] = lax.dot_general(
            gather,
            queries[:, h].reshape(SLOTS, HD).astype(jnp.bfloat16),
            (((0,), (0,)), ((), ())),
            preferred_element_type=jnp.float32,
        ).astype(jnp.bfloat16)
    mixed_scr[...] = jnp.zeros_like(mixed_scr)
    stat_scr[...] = jnp.zeros_like(stat_scr)

    @pl.loop(0, (count + span - 1) // span)
    def _(index):
        start = pl.multiple_of(index * span, span)
        query = query_scr[:, pl.ds(start, span), :].reshape(block, HD)
        peak = jnp.full((block, HD), -jnp.inf, jnp.float32)
        for n, piece in enumerate(pieces):
            scores = lax.dot_general(
                query, piece[0], (((1,), (1,)), ((), ())), preferred_element_type=jnp.float32
            )
            score_ref[n] = scores
            peak = jnp.maximum(peak, jnp.maximum(scores[:, :HD], scores[:, HD:]))
        peak = jnp.max(peak, axis=1, keepdims=True)
        total = jnp.zeros((block, HD), jnp.float32)
        mixed = jnp.zeros((block, HD), jnp.float32)
        for n, piece in enumerate(pieces):
            weights = jnp.exp2((score_ref[n] - peak) * (SCALE * LOG2E))
            total = total + (weights[:, :HD] + weights[:, HD:])
            mixed = mixed + jnp.dot(
                weights.astype(jnp.bfloat16), piece[1], preferred_element_type=jnp.float32
            )
        total = jnp.sum(total, axis=1, keepdims=True)
        mixed_scr[:, pl.ds(start, span), :] = (mixed / total).astype(jnp.bfloat16).reshape(RATIO, span, HD)
        lse = peak * SCALE + jnp.log(total)
        stat_scr[pl.ds(start, span), :] = split_stat(lse.reshape(RATIO, span, 1), span).astype(jnp.bfloat16)

    idle = 1.0 - valid
    mean = sum(piece[1].astype(jnp.float32).reshape(PIECE // 8, 8, HD).sum(axis=0) for piece in pieces)
    mean = jnp.sum(mean, axis=0, keepdims=True) / tokens
    heads = []
    for h in range(RATIO):
        spread_out = jnp.dot(gather, mixed_scr[h], preferred_element_type=jnp.float32) + idle * mean
        heads.append(spread_out.reshape(32, 8, HD))
    for h in range(0, RATIO, 2):
        out_ref[:, h * 8 : h * 8 + 16] = jnp.concatenate(heads[h : h + 2], axis=1).astype(jnp.bfloat16)
    even = split_stat(jnp.full((RATIO, SLOTS, 1), math.log(tokens), jnp.float32), SLOTS)
    stat = jnp.dot(gather, stat_scr[...], preferred_element_type=jnp.float32) + idle * even
    stat = stat.reshape(32, 8, HD)
    out_ref[:, 64:] = jnp.concatenate([stat, jnp.zeros_like(stat)], axis=1).astype(jnp.bfloat16)


def split_stat(lse, span):
    high = lse.astype(jnp.bfloat16).astype(jnp.float32)
    rest = lse - high
    middle = rest.astype(jnp.bfloat16).astype(jnp.float32)
    low = rest - middle
    lane = lax.broadcasted_iota(jnp.int32, (span, HD), 1)
    stat = jnp.zeros((span, HD), jnp.float32)
    for h in range(RATIO):
        for n, part in enumerate((high, middle, low)):
            stat = jnp.where(lane == n * 8 + h, part[h], stat)
    return stat


def select_kernel(got_ref, back_ref, *refs):
    send_ref = refs[-1]
    tags = [got_ref[y, 64:].astype(jnp.float32)[8:, :1].astype(jnp.int32) for y in range(KVH)]
    lane = lax.broadcasted_iota(jnp.int32, (1, ROWS), 1)
    lane_key = ((lane >> 1) & 3) * 512 + ((lane >> 3) & 7) * 64 + (lane >> 6) * 2 + (lane & 1)
    tag = jnp.concatenate([tags[y] for y in range(KVH) for _ in range(RATIO)], axis=0)
    row_key = (lax.broadcasted_iota(jnp.int32, (256, 1), 0) >> 3) * 64 + tag
    select = (row_key == lane_key).astype(jnp.float32).astype(jnp.bfloat16)
    far = jnp.dot(select, back_ref[:, :64].reshape(ROWS, HD), preferred_element_type=jnp.float32)
    send_ref[:, :64] = far.astype(jnp.bfloat16).reshape(KVH, 64, HD)
    stats = back_ref[:, 64:].astype(jnp.float32)[:, :8].reshape(SLOTS, HD).astype(jnp.bfloat16)
    lane = lax.broadcasted_iota(jnp.int32, (1, SLOTS), 1)
    lane_key = ((lane >> 1) & 3) * 64 + (lane >> 3) * 2 + (lane & 1)
    row_key = (lax.broadcasted_iota(jnp.int32, (32, 1), 0) >> 3) * 64 + jnp.concatenate(tags, axis=0)
    select = (row_key == lane_key).astype(jnp.float32).astype(jnp.bfloat16)
    stat = jnp.dot(select, stats, preferred_element_type=jnp.float32).reshape(KVH, 8, HD)
    send_ref[:, 64:] = jnp.concatenate([stat, jnp.zeros_like(stat)], axis=1).astype(jnp.bfloat16)


def merge_kernel(back_ref, near_ref, out_ref):
    lane = lax.broadcasted_iota(jnp.int32, (HELD, HD), 1)
    for y in range(KVH):
        far = back_ref[y, :64].astype(jnp.float32)
        stat = jnp.where(lane < 24, back_ref[y, 64:].astype(jnp.float32)[:8], 0.0)
        for h in range(RATIO):
            head = y * RATIO + h
            far_lse = jnp.sum(jnp.where((lane & 7) == h, stat, 0.0), axis=1, keepdims=True)
            near_lse = near_ref[HEADS + head]
            top = jnp.maximum(far_lse, near_lse)
            far_scale = jnp.exp(far_lse - top)
            near_scale = jnp.exp(near_lse - top)
            merged = far[h * 8 : (h + 1) * 8] * far_scale + near_ref[head] * near_scale
            out_ref[:, head * HD : (head + 1) * HD] = (merged / (far_scale + near_scale)).astype(
                jnp.bfloat16
            )


VMEM = pl.BlockSpec(memory_space=pltpu.VMEM)
SMEM = pl.BlockSpec(memory_space=pltpu.SMEM)
ANY = pl.BlockSpec(memory_space=pl.ANY)


def params(mib):
    return pltpu.CompilerParams(vmem_limit_bytes=mib << 20)


def shards(
    prompt_of,
    suffix_len,
    query,
    new_key,
    new_value,
    suffix_key,
    suffix_value,
    prefix_key,
    prefix_value,
):
    place = lax.axis_index(NEAR).astype(jnp.int32).reshape(1)
    sent, *cuts = pl.pallas_call(
        prep_kernel,
        out_shape=[jax.ShapeDtypeStruct((KVH, 80, HD), jnp.bfloat16)]
        + [jax.ShapeDtypeStruct((2, PIECE, HD), jnp.bfloat16)] * 8,
        in_specs=[SMEM, ANY, ANY, ANY, ANY],
        out_specs=[VMEM] * 9,
        scratch_shapes=[
            pltpu.SMEM((HELD,), jnp.int32),
            pltpu.VMEM((HELD, HEADS * HD), jnp.bfloat16),
            pltpu.SemaphoreType.DMA((2,)),
            pltpu.SemaphoreType.DMA((8, 2)),
        ],
        compiler_params=params(60),
        name="prep",
    )(place, prompt_of, query, prefix_key, prefix_value)
    held = [cuts[0]]
    for step in range(1, 8):
        held.append(lax.ppermute(cuts[step], NEAR, [(i, i ^ step) for i in range(8)]))
    swapped = [lax.ppermute(piece, "c", [(0, 1), (1, 0)]) for piece in held]
    got = lax.all_to_all(sent, "y", 0, 0, tiled=True)
    outgoing = pl.pallas_call(
        pack_kernel,
        out_shape=jax.ShapeDtypeStruct((ROWS, HD), jnp.bfloat16),
        in_specs=[VMEM] + [ANY] * 3,
        out_specs=VMEM,
        compiler_params=params(8),
        name="pack",
    )(got, *held[4:7])
    arrived = lax.all_to_all(outgoing.reshape(PROMPTS, 64, HD), FAR, 0, 0, tiled=True)

    near = pl.pallas_call(
        near_kernel,
        grid=(HELD,),
        out_shape=jax.ShapeDtypeStruct((2 * HEADS, HELD, HD), jnp.float32),
        in_specs=[
            SMEM,
            pl.BlockSpec((HELD, HEADS * HD), lambda i: (0, 0)),
            pl.BlockSpec((HELD, KVH * HD), lambda i: (0, 0)),
            pl.BlockSpec((HELD, KVH * HD), lambda i: (0, 0)),
            pl.BlockSpec((1, SUF, KVH * HD), lambda i: (i, 0, 0)),
            pl.BlockSpec((1, SUF, KVH * HD), lambda i: (i, 0, 0)),
        ],
        out_specs=pl.BlockSpec((2 * HEADS, HELD, HD), lambda i: (0, 0, 0)),
        scratch_shapes=[pltpu.VMEM((HEADS, HELD, HD), jnp.float32)],
        compiler_params=params(60),
        cost_estimate=pl.CostEstimate(flops=300_000_000, bytes_accessed=4_500_000, transcendentals=65536),
        name="near",
    )(
        suffix_len,
        query,
        new_key,
        new_value,
        suffix_key,
        suffix_value,
    )

    parcel = pl.pallas_call(
        far_kernel,
        out_shape=jax.ShapeDtypeStruct((PROMPTS, 80, HD), jnp.bfloat16),
        in_specs=[VMEM] * 17,
        out_specs=VMEM,
        scratch_shapes=[
            pltpu.VMEM((16, 256, PIECE), jnp.float32),
            pltpu.VMEM((RATIO, SLOTS, HD), jnp.bfloat16),
            pltpu.VMEM((RATIO, SLOTS, HD), jnp.bfloat16),
            pltpu.VMEM((SLOTS, HD), jnp.bfloat16),
        ],
        compiler_params=params(16),
        name="far",
    )(arrived.reshape(ROWS, HD), *held, *swapped)
    back = lax.all_to_all(parcel, FAR, 0, 0, tiled=True)
    chosen = pl.pallas_call(
        select_kernel,
        out_shape=jax.ShapeDtypeStruct((KVH, 80, HD), jnp.bfloat16),
        in_specs=[VMEM] * 2,
        out_specs=VMEM,
        compiler_params=params(8),
        name="select",
    )(got, back)
    final = lax.all_to_all(chosen, "y", 0, 0, tiled=True)
    return pl.pallas_call(
        merge_kernel,
        out_shape=jax.ShapeDtypeStruct((HELD, HEADS * HD), jnp.bfloat16),
        in_specs=[VMEM] * 2,
        out_specs=VMEM,
        compiler_params=params(12),
        name="merge",
    )(final, near)


def solution(mesh):
    fine = Mesh(mesh.devices.reshape(2, 8, 2, 4, 2), ALL)
    grp = ("xh", "z")
    blk = ("xl", "y", "c")
    in_specs = (
        P(ALL),
        P(ALL),
        P(ALL, None),
        P(ALL, None),
        P(ALL, None),
        P(ALL, None, None),
        P(ALL, None, None),
        P(grp, blk, None),
        P(grp, blk, None),
    )
    return jax.shard_map(
        shards, mesh=fine, in_specs=in_specs, out_specs=P(ALL, None), check_vma=False
    )
```

profile of v0, /device:TPU:32, one launch (start us, length us, event | category | flops | bytes accessed | tf_op | source)
XLA Modules:
  0.0 98.2 jit_solution(5343612569261663051)
XLA Ops:
  0.0 2.5 %prep.1 = (bf16[4,80,128]{2,1,0:T(8,128)(2,1)}, bf16[2,256,128]{2,1,0:T(8,128)(2,1)}, bf16[2,256,128]{2,1,0:T(8,128)(2,1)}, bf16[2,256,128]{2,1,0:T(8,128)(2,1)}...) custom-call(s32[1]{0:T(128)} %bitcast.place_ref, ...), custom_call_target="tpu_custom_call" | custom-call | tf_op jit(solution)/shard_map/prep/pallas_call | solution.py:310
  2.6 1.6 %collective-permute-start = (bf16[2,256,128]{2,1,0:T(8,128)(2,1)}, bf16[2,256,128]{2,1,0:T(8,128)(2,1)S(1)}, u32[]{:S(2)}, u32[]{:S(2)}) collective-permute-start(bf16[2,256,128]{2,1,0:T(8,128)(2,1)} %get-tuple-element.15), channel_id=1, source_target_pairs={{0,8},{2,10},{4,12},{6,14},{8,0},{10,2},{12,4},{14,6},{1,9},{3,11}... | collective-permute-start | bytes 393224 | tf_op jit(solution)/shard_map/ppermute | solution.py:327
  4.1 1.5 %collective-permute-start.1 = (bf16[2,256,128]{2,1,0:T(8,128)(2,1)}, bf16[2,256,128]{2,1,0:T(8,128)(2,1)S(1)}, u32[]{:S(2)}, u32[]{:S(2)}) collective-permute-start(bf16[2,256,128]{2,1,0:T(8,128)(2,1)} %get-tuple-element.16), channel_id=1, source_target_pairs={{0,10},{2,8},{4,14},{6,12},{8,2},{10,0},{12,6},{14,4},{1,11},{3,9}... | collective-permute-start | bytes 393224 | tf_op jit(solution)/shard_map/ppermute | solution.py:327
  5.7 3.8 %collective-permute-start.2 = (bf16[2,256,128]{2,1,0:T(8,128)(2,1)}, bf16[2,256,128]{2,1,0:T(8,128)(2,1)S(1)}, u32[]{:S(2)}, u32[]{:S(2)}) collective-permute-start(bf16[2,256,128]{2,1,0:T(8,128)(2,1)} %get-tuple-element.17), channel_id=1, source_target_pairs={{0,12},{2,14},{4,8},{6,10},{8,4},{10,6},{12,0},{14,2},{1,13},{3,15... | collective-permute-start | bytes 393224 | tf_op jit(solution)/shard_map/ppermute | solution.py:327
  9.5 9.0 %all_to_all.20.got_ref = bf16[4,80,128]{2,1,0:T(8,128)(2,1)S(1)} all-to-all(bf16[4,80,128]{2,1,0:T(8,128)(2,1)} %get-tuple-element.14), channel_id=1, replica_groups=mesh['xh'=2,'z'=8,'xl'=2,'y'=4,'c'=2] {'y'}, dimensions={0} | all-to-all | bytes 163840 | tf_op jit(solution)/shard_map/all_to_all | solution.py:329
  18.5 1.5 %pack.1 = bf16[2048,128]{1,0:T(8,128)(2,1)} custom-call(bf16[4,80,128]{2,1,0:T(8,128)(2,1)S(1)} %all_to_all.20.got_ref, bf16[2,256,128]{2,1,0:T(8,128)(2,1)S(1)} %collective-permute-done.refs_0_.refs_4_, bf16[2,256,128]{2,1,0:T(8,128)(2,1)S(1)} %collective-permute-done.1.refs_1_.refs_5_, bf16[2,256,128]{2,1,0:T(8,128)(2,1)S(1)} %collective-permute-done.2.refs_2_.refs_6_), custom_call_target="tpu_custom_call" | custom-call | tf_op jit(solution)/shard_map/pack/pallas_call | solution.py:330
  20.0 10.9 %all-to-all-start.1 = ((bf16[32,64,128]{2,1,0:T(8,128)(2,1)}), bf16[32,64,128]{2,1,0:T(8,128)(2,1)S(1)}, u32[]{:S(2)}, u32[]{:S(2)}) async-start(bf16[32,64,128]{2,1,0:T(8,128)(2,1)} %bitcast.1), calls=%async_computation.1 | async-start | bytes 1048576 | tf_op jit(solution)/shard_map/all_to_all | solution.py:338
  30.9 1.3 %collective-permute-start.5 = (bf16[2,256,128]{2,1,0:T(8,128)(2,1)S(1)}, bf16[2,256,128]{2,1,0:T(8,128)(2,1)S(1)}, u32[]{:S(2)}, u32[]{:S(2)}) collective-permute-start(bf16[2,256,128]{2,1,0:T(8,128)(2,1)S(1)} %copy-done.5), channel_id=1, source_target_pairs={{0,6},{2,4},{4,2},{6,0},{8,14},{10,12},{12,10},{14,8},{1,7},{3,5},... | collective-permute-start | bytes 393224 | tf_op jit(solution)/shard_map/ppermute | solution.py:327
  32.2 3.0 %collective-permute-start.6 = (bf16[2,256,128]{2,1,0:T(8,128)(2,1)S(1)}, bf16[2,256,128]{2,1,0:T(8,128)(2,1)S(1)}, u32[]{:S(2)}, u32[]{:S(2)}) collective-permute-start(bf16[2,256,128]{2,1,0:T(8,128)(2,1)S(1)} %copy-done.4), channel_id=1, source_target_pairs={{0,14},{2,12},{4,10},{6,8},{8,6},{10,4},{12,2},{14,0},{1,15},{3,13... | collective-permute-start | bytes 393224 | tf_op jit(solution)/shard_map/ppermute | solution.py:327
  35.1 2.6 %collective-permute-start.4 = (bf16[2,256,128]{2,1,0:T(8,128)(2,1)S(1)}, bf16[2,256,128]{2,1,0:T(8,128)(2,1)S(1)}, u32[]{:S(2)}, u32[]{:S(2)}) collective-permute-start(bf16[2,256,128]{2,1,0:T(8,128)(2,1)S(1)} %copy-done.2), channel_id=1, source_target_pairs={{0,4},{2,6},{4,0},{6,2},{8,12},{10,14},{12,8},{14,10},{1,5},{3,7},... | collective-permute-start | bytes 393224 | tf_op jit(solution)/shard_map/ppermute | solution.py:327
  37.8 0.0 collective-permute-start.7
  37.8 4.8 %collective-permute-done.5.refs_3_ = bf16[2,256,128]{2,1,0:T(8,128)(2,1)S(1)} collective-permute-done((bf16[2,256,128]{2,1,0:T(8,128)(2,1)S(1)}, bf16[2,256,128]{2,1,0:T(8,128)(2,1)S(1)}, u32[]{:S(2)}, u32[]{:S(2)}) %collective-permute-start.5) | collective-permute-done | bytes 131104 | tf_op jit(solution)/shard_map/ppermute | solution.py:327
  42.6 0.5 collective-permute-start.12
  43.1 0.1 collective-permute-start.13
  43.2 0.4 collective-permute-start.10
  43.6 0.1 collective-permute-start.14
  43.7 0.2 collective-permute-done.11.refs_12_
  44.0 0.2 collective-permute-start.8
  44.2 0.3 collective-permute-start.9
  44.5 0.0 collective-permute-done.13.refs_14_
  44.5 0.2 collective-permute-done.10.refs_11_
  44.7 0.3 collective-permute-done.14.refs_15_
  45.0 0.3 collective-permute-done.8.refs_9_
  45.3 0.2 collective-permute-done.9.refs_10_
  45.5 2.3 %all-to-all-done.1 = bf16[32,64,128]{2,1,0:T(8,128)(2,1)S(1)} async-done(((bf16[32,64,128]{2,1,0:T(8,128)(2,1)}), bf16[32,64,128]{2,1,0:T(8,128)(2,1)S(1)}, u32[]{:S(2)}, u32[]{:S(2)}) %all-to-all-start.1) | async-done | bytes 524320 | tf_op jit(solution)/shard_map/all_to_all | solution.py:338
  47.9 3.4 %far.1 = bf16[32,80,128]{2,1,0:T(8,128)(2,1)S(1)} custom-call(bf16[2048,128]{1,0:T(8,128)(2,1)S(1)} %bitcast.3, bf16[2,256,128]{2,1,0:T(8,128)(2,1)S(1)} %copy-done.1, bf16[2,256,128]{2,1,0:T(8,128)(2,1)S(1)} %collective-permute-done.3.refs_1_, bf16[2,256,128]{2,1,0:T(8,128)(2,1)S(1)} %collective-permute-done.4.refs_2_, ...), custom_call_target="tpu_custom_call" | custom-call | tf_op jit(solution)/shard_map/far/pallas_call | solution.py:366
  51.3 33.6 %all_to_all.21.back_ref = bf16[32,80,128]{2,1,0:T(8,128)(2,1)S(1)} all-to-all(bf16[32,80,128]{2,1,0:T(8,128)(2,1)S(1)} %far.1), channel_id=1, replica_groups=mesh['xh'=2,'z'=8,'xl'=2,'y'=4,'c'=2] {'xh','z','xl'}, dimensions={0} | all-to-all | bytes 1310720 | tf_op jit(solution)/shard_map/all_to_all | solution.py:380
  84.8 1.1 %select.1 = bf16[4,80,128]{2,1,0:T(8,128)(2,1)} custom-call(bf16[4,80,128]{2,1,0:T(8,128)(2,1)S(1)} %all_to_all.20.got_ref, bf16[32,80,128]{2,1,0:T(8,128)(2,1)S(1)} %all_to_all.21.back_ref), custom_call_target="tpu_custom_call" | custom-call | tf_op jit(solution)/shard_map/select/pallas_call | solution.py:381
  86.0 3.3 %all-to-all-start.3 = ((bf16[4,80,128]{2,1,0:T(8,128)(2,1)}), bf16[4,80,128]{2,1,0:T(8,128)(2,1)S(1)}, u32[]{:S(2)}, u32[]{:S(2)}) async-start(bf16[4,80,128]{2,1,0:T(8,128)(2,1)} %select.1), calls=%async_computation.3 | async-start | bytes 163840 | tf_op jit(solution)/shard_map/all_to_all | solution.py:389
  89.3 7.2 %near.1.near_ref = f32[64,8,128]{2,1,0:T(8,128)} custom-call(s32[8]{0:T(128)} %len_ref.1, bf16[8,4096]{1,0:T(8,128)(2,1)} %query_ref.1, bf16[8,512]{1,0:T(8,128)(2,1)} %new_key_ref.1, bf16[8,512]{1,0:T(8,128)(2,1)} %new_value_ref.1, bf16[8,256,512]{2,1,0:T(8,128)(2,1)} %key_ref.3, bf16[8,256,512]{2,1,0:T(8,128)(2,1)} %value_ref.3), custom_call_target="tpu_custom_call" | custom-call | flops 300000000 | bytes 4500000 | tf_op jit(solution)/shard_map/near/pallas_call | solution.py:340
  96.4 0.9 copy-done
  97.4 0.8 merge.1
  (22 shorter events, 0.1 us)
Async XLA Ops:
  2.5 28.4 %copy-start.5 = (bf16[2,256,128]{2,1,0:T(8,128)(2,1)S(1)}, bf16[2,256,128]{2,1,0:T(8,128)(2,1)}, u32[]{:S(2)}) copy-start(bf16[2,256,128]{2,1,0:T(8,128)(2,1)} %get-tuple-element.21) | copy-start | bytes 393220
  2.5 29.6 %copy-start.4 = (bf16[2,256,128]{2,1,0:T(8,128)(2,1)S(1)}, bf16[2,256,128]{2,1,0:T(8,128)(2,1)}, u32[]{:S(2)}) copy-start(bf16[2,256,128]{2,1,0:T(8,128)(2,1)} %get-tuple-element.22) | copy-start | bytes 393220
  2.5 32.6 %copy-start.3 = (bf16[2,256,128]{2,1,0:T(8,128)(2,1)S(1)}, bf16[2,256,128]{2,1,0:T(8,128)(2,1)}, u32[]{:S(2)}) copy-start(bf16[2,256,128]{2,1,0:T(8,128)(2,1)} %get-tuple-element.19) | copy-start | bytes 393220
  2.5 32.6 %copy-start.2 = (bf16[2,256,128]{2,1,0:T(8,128)(2,1)S(1)}, bf16[2,256,128]{2,1,0:T(8,128)(2,1)}, u32[]{:S(2)}) copy-start(bf16[2,256,128]{2,1,0:T(8,128)(2,1)} %get-tuple-element.20) | copy-start | bytes 393220
  2.6 35.2 %copy-start.1 = (bf16[2,256,128]{2,1,0:T(8,128)(2,1)S(1)}, bf16[2,256,128]{2,1,0:T(8,128)(2,1)}, u32[]{:S(2)}) copy-start(bf16[2,256,128]{2,1,0:T(8,128)(2,1)} %get-tuple-element.18.refs_0_) | copy-start | bytes 393220
  2.6 15.9 %collective-permute-start = (bf16[2,256,128]{2,1,0:T(8,128)(2,1)}, bf16[2,256,128]{2,1,0:T(8,128)(2,1)S(1)}, u32[]{:S(2)}, u32[]{:S(2)}) collective-permute-start(bf16[2,256,128]{2,1,0:T(8,128)(2,1)} %get-tuple-element.15), channel_id=1, source_target_pairs={{0,8},{2,10},{4,12},{6,14},{8,0},{10,2},{12,4},{14,6},{1,9},{3,11}... | collective-permute-start | bytes 393224 | tf_op jit(solution)/shard_map/ppermute | solution.py:327
  4.1 14.4 %collective-permute-start.1 = (bf16[2,256,128]{2,1,0:T(8,128)(2,1)}, bf16[2,256,128]{2,1,0:T(8,128)(2,1)S(1)}, u32[]{:S(2)}, u32[]{:S(2)}) collective-permute-start(bf16[2,256,128]{2,1,0:T(8,128)(2,1)} %get-tuple-element.16), channel_id=1, source_target_pairs={{0,10},{2,8},{4,14},{6,12},{8,2},{10,0},{12,6},{14,4},{1,11},{3,9}... | collective-permute-start | bytes 393224 | tf_op jit(solution)/shard_map/ppermute | solution.py:327
  5.7 12.8 %collective-permute-start.2 = (bf16[2,256,128]{2,1,0:T(8,128)(2,1)}, bf16[2,256,128]{2,1,0:T(8,128)(2,1)S(1)}, u32[]{:S(2)}, u32[]{:S(2)}) collective-permute-start(bf16[2,256,128]{2,1,0:T(8,128)(2,1)} %get-tuple-element.17), channel_id=1, source_target_pairs={{0,12},{2,14},{4,8},{6,10},{8,4},{10,6},{12,0},{14,2},{1,13},{3,15... | collective-permute-start | bytes 393224 | tf_op jit(solution)/shard_map/ppermute | solution.py:327
  20.0 27.9 %all-to-all-start.1 = ((bf16[32,64,128]{2,1,0:T(8,128)(2,1)}), bf16[32,64,128]{2,1,0:T(8,128)(2,1)S(1)}, u32[]{:S(2)}, u32[]{:S(2)}) async-start(bf16[32,64,128]{2,1,0:T(8,128)(2,1)} %bitcast.1), calls=%async_computation.1 | async-start | bytes 1048576 | tf_op jit(solution)/shard_map/all_to_all | solution.py:338
  30.9 11.7 %collective-permute-start.5 = (bf16[2,256,128]{2,1,0:T(8,128)(2,1)S(1)}, bf16[2,256,128]{2,1,0:T(8,128)(2,1)S(1)}, u32[]{:S(2)}, u32[]{:S(2)}) collective-permute-start(bf16[2,256,128]{2,1,0:T(8,128)(2,1)S(1)} %copy-done.5), channel_id=1, source_target_pairs={{0,6},{2,4},{4,2},{6,0},{8,14},{10,12},{12,10},{14,8},{1,7},{3,5},... | collective-permute-start | bytes 393224 | tf_op jit(solution)/shard_map/ppermute | solution.py:327
  32.2 10.4 %collective-permute-start.6 = (bf16[2,256,128]{2,1,0:T(8,128)(2,1)S(1)}, bf16[2,256,128]{2,1,0:T(8,128)(2,1)S(1)}, u32[]{:S(2)}, u32[]{:S(2)}) collective-permute-start(bf16[2,256,128]{2,1,0:T(8,128)(2,1)S(1)} %copy-done.4), channel_id=1, source_target_pairs={{0,14},{2,12},{4,10},{6,8},{8,6},{10,4},{12,2},{14,0},{1,15},{3,13... | collective-permute-start | bytes 393224 | tf_op jit(solution)/shard_map/ppermute | solution.py:327
  35.1 8.0 %collective-permute-start.3 = (bf16[2,256,128]{2,1,0:T(8,128)(2,1)S(1)}, bf16[2,256,128]{2,1,0:T(8,128)(2,1)S(1)}, u32[]{:S(2)}, u32[]{:S(2)}) collective-permute-start(bf16[2,256,128]{2,1,0:T(8,128)(2,1)S(1)} %copy-done.3), channel_id=1, source_target_pairs={{0,2},{2,0},{4,6},{6,4},{8,10},{10,8},{12,14},{14,12},{1,3},{3,1},... | collective-permute-start | bytes 393224 | tf_op jit(solution)/shard_map/ppermute | solution.py:327
  35.1 8.1 %collective-permute-start.4 = (bf16[2,256,128]{2,1,0:T(8,128)(2,1)S(1)}, bf16[2,256,128]{2,1,0:T(8,128)(2,1)S(1)}, u32[]{:S(2)}, u32[]{:S(2)}) collective-permute-start(bf16[2,256,128]{2,1,0:T(8,128)(2,1)S(1)} %copy-done.2), channel_id=1, source_target_pairs={{0,4},{2,6},{4,0},{6,2},{8,12},{10,14},{12,8},{14,10},{1,5},{3,7},... | collective-permute-start | bytes 393224 | tf_op jit(solution)/shard_map/ppermute | solution.py:327
  37.8 5.9 %collective-permute-start.7 = (bf16[2,256,128]{2,1,0:T(8,128)(2,1)S(1)}, bf16[2,256,128]{2,1,0:T(8,128)(2,1)S(1)}, u32[]{:S(2)}, u32[]{:S(2)}) collective-permute-start(bf16[2,256,128]{2,1,0:T(8,128)(2,1)S(1)} %copy-done.1), channel_id=1, source_target_pairs={{0,1},{1,0},{2,3},{3,2},{4,5},{5,4},{6,7},{7,6},{8,9},{9,8},{10,11... | collective-permute-start | bytes 393224 | tf_op jit(solution)/shard_map/ppermute | solution.py:328
  42.6 1.3 %collective-permute-start.11 = (bf16[2,256,128]{2,1,0:T(8,128)(2,1)S(1)}, bf16[2,256,128]{2,1,0:T(8,128)(2,1)S(1)}, u32[]{:S(2)}, u32[]{:S(2)}) collective-permute-start(bf16[2,256,128]{2,1,0:T(8,128)(2,1)S(1)} %collective-permute-done.refs_0_.refs_4_), channel_id=1, source_target_pairs={{0,1},{1,0},{2,3},{3,2},{4,5},{5,4},{6,7},{7,6},{8,9},{9,8},{10,11... | collective-permute-start | bytes 393224 | tf_op jit(solution)/shard_map/ppermute | solution.py:328
  42.6 1.5 %collective-permute-start.12 = (bf16[2,256,128]{2,1,0:T(8,128)(2,1)S(1)}, bf16[2,256,128]{2,1,0:T(8,128)(2,1)S(1)}, u32[]{:S(2)}, u32[]{:S(2)}) collective-permute-start(bf16[2,256,128]{2,1,0:T(8,128)(2,1)S(1)} %collective-permute-done.1.refs_1_.refs_5_), channel_id=1, source_target_pairs={{0,1},{1,0},{2,3},{3,2},{4,5},{5,4},{6,7},{7,6},{8,9},{9,8},{10,11... | collective-permute-start | bytes 393224 | tf_op jit(solution)/shard_map/ppermute | solution.py:328
  43.1 1.3 %collective-permute-start.13 = (bf16[2,256,128]{2,1,0:T(8,128)(2,1)S(1)}, bf16[2,256,128]{2,1,0:T(8,128)(2,1)S(1)}, u32[]{:S(2)}, u32[]{:S(2)}) collective-permute-start(bf16[2,256,128]{2,1,0:T(8,128)(2,1)S(1)} %collective-permute-done.2.refs_2_.refs_6_), channel_id=1, source_target_pairs={{0,1},{1,0},{2,3},{3,2},{4,5},{5,4},{6,7},{7,6},{8,9},{9,8},{10,11... | collective-permute-start | bytes 393224 | tf_op jit(solution)/shard_map/ppermute | solution.py:328
  43.2 1.4 %collective-permute-start.10 = (bf16[2,256,128]{2,1,0:T(8,128)(2,1)S(1)}, bf16[2,256,128]{2,1,0:T(8,128)(2,1)S(1)}, u32[]{:S(2)}, u32[]{:S(2)}) collective-permute-start(bf16[2,256,128]{2,1,0:T(8,128)(2,1)S(1)} %collective-permute-done.5.refs_3_), channel_id=1, source_target_pairs={{0,1},{1,0},{2,3},{3,2},{4,5},{5,4},{6,7},{7,6},{8,9},{9,8},{10,11... | collective-permute-start | bytes 393224 | tf_op jit(solution)/shard_map/ppermute | solution.py:328
  43.6 1.3 %collective-permute-start.14 = (bf16[2,256,128]{2,1,0:T(8,128)(2,1)S(1)}, bf16[2,256,128]{2,1,0:T(8,128)(2,1)S(1)}, u32[]{:S(2)}, u32[]{:S(2)}) collective-permute-start(bf16[2,256,128]{2,1,0:T(8,128)(2,1)S(1)} %collective-permute-done.6.refs_7_), channel_id=1, source_target_pairs={{0,1},{1,0},{2,3},{3,2},{4,5},{5,4},{6,7},{7,6},{8,9},{9,8},{10,11... | collective-permute-start | bytes 393224 | tf_op jit(solution)/shard_map/ppermute | solution.py:328
  44.0 1.3 %collective-permute-start.8 = (bf16[2,256,128]{2,1,0:T(8,128)(2,1)S(1)}, bf16[2,256,128]{2,1,0:T(8,128)(2,1)S(1)}, u32[]{:S(2)}, u32[]{:S(2)}) collective-permute-start(bf16[2,256,128]{2,1,0:T(8,128)(2,1)S(1)} %collective-permute-done.3.refs_1_), channel_id=1, source_target_pairs={{0,1},{1,0},{2,3},{3,2},{4,5},{5,4},{6,7},{7,6},{8,9},{9,8},{10,11... | collective-permute-start | bytes 393224 | tf_op jit(solution)/shard_map/ppermute | solution.py:328
  44.2 1.3 %collective-permute-start.9 = (bf16[2,256,128]{2,1,0:T(8,128)(2,1)S(1)}, bf16[2,256,128]{2,1,0:T(8,128)(2,1)S(1)}, u32[]{:S(2)}, u32[]{:S(2)}) collective-permute-start(bf16[2,256,128]{2,1,0:T(8,128)(2,1)S(1)} %collective-permute-done.4.refs_2_), channel_id=1, source_target_pairs={{0,1},{1,0},{2,3},{3,2},{4,5},{5,4},{6,7},{7,6},{8,9},{9,8},{10,11... | collective-permute-start | bytes 393224 | tf_op jit(solution)/shard_map/ppermute | solution.py:328
  86.0 10.5 %all-to-all-start.3 = ((bf16[4,80,128]{2,1,0:T(8,128)(2,1)}), bf16[4,80,128]{2,1,0:T(8,128)(2,1)S(1)}, u32[]{:S(2)}, u32[]{:S(2)}) async-start(bf16[4,80,128]{2,1,0:T(8,128)(2,1)} %select.1), calls=%async_computation.3 | async-start | bytes 163840 | tf_op jit(solution)/shard_map/all_to_all | solution.py:389
  96.4 1.0 copy-start
where the time goes:
time: 98.7 us; the launch traced here: 98.2 us
  blocking collectives  42.6 us (43%)
  starting transfers between devices  29.6 us (30%)
  Pallas kernels  16.4 us (17%)
  waiting for transfers between devices  8.46 us (9%)
    all_to_all x1, blocking collectives, shards(): back = lax.all_to_all(parcel, FAR, 0, 0, tiled=True)  33.6 us
    ppermute x7, starting transfers between devices, shards(): lax.ppermute(cuts[step], NEAR, [(i, i ^ step) for i in range(8)])  13.8 us
    all_to_all x1, starting transfers between devices, shards(): lax.all_to_all(outgoing.reshape(PROMPTS, 64, HD), FAR, 0, 0, tiled=True)  10.9 us
    all_to_all x1, blocking collectives, shards(): got = lax.all_to_all(sent, 'y', 0, 0, tiled=True)  8.97 us
    pallas_call x1, Pallas kernels, shards(): pl.pallas_call(near_kernel, grid=(HELD,), out_shape=jax.ShapeDtypeStruct(...  7.16 us
    ppermute x7, waiting for transfers between devices, shards(): lax.ppermute(cuts[step], NEAR, [(i, i ^ step) for i in range(8)])  4.84 us
    pallas_call x1, Pallas kernels, shards(): pl.pallas_call(far_kernel, out_shape=jax.ShapeDtypeStruct((PROMPTS, 80, H...  3.39 us
    all_to_all x1, starting transfers between devices, shards(): final = lax.all_to_all(chosen, 'y', 0, 0, tiled=True)  3.29 us
  transfers between devices with their start and end apart: 17, of which 7 were waited for; matrix products, arithmetic and copies ran while one was open for 0% of the time, Pallas kernels for 7%

commit v1 on v0

--- a/solution.py
+++ b/solution.py
@@ -171,8 +171,6 @@
 def far_kernel(query_ref, *refs):
     pieces = refs[:16]
     out_ref, score_ref, query_scr, mixed_scr, stat_scr = refs[16:]
-    span = 32
-    block = span * RATIO
     tokens = 16 * PIECE
     queries = query_ref[...].astype(jnp.float32).reshape(32, RATIO, 8, HD)
     biggest = jnp.max(jnp.max(jnp.abs(queries), axis=1).reshape(SLOTS, HD), axis=1, keepdims=True)
@@ -196,22 +194,21 @@
     mixed_scr[...] = jnp.zeros_like(mixed_scr)
     stat_scr[...] = jnp.zeros_like(stat_scr)
 
-    @pl.loop(0, (count + span - 1) // span)
-    def _(index):
-        start = pl.multiple_of(index * span, span)
+    def work(start, span):
+        block = span * RATIO
         query = query_scr[:, pl.ds(start, span), :].reshape(block, HD)
         peak = jnp.full((block, HD), -jnp.inf, jnp.float32)
         for n, piece in enumerate(pieces):
             scores = lax.dot_general(
                 query, piece[0], (((1,), (1,)), ((), ())), preferred_element_type=jnp.float32
             )
-            score_ref[n] = scores
+            score_ref[n, :block] = scores
             peak = jnp.maximum(peak, jnp.maximum(scores[:, :HD], scores[:, HD:]))
         peak = jnp.max(peak, axis=1, keepdims=True)
         total = jnp.zeros((block, HD), jnp.float32)
         mixed = jnp.zeros((block, HD), jnp.float32)
         for n, piece in enumerate(pieces):
-            weights = jnp.exp2((score_ref[n] - peak) * (SCALE * LOG2E))
+            weights = jnp.exp2((score_ref[n, :block] - peak) * (SCALE * LOG2E))
             total = total + (weights[:, :HD] + weights[:, HD:])
             mixed = mixed + jnp.dot(
                 weights.astype(jnp.bfloat16), piece[1], preferred_element_type=jnp.float32
@@ -220,6 +217,16 @@
         mixed_scr[:, pl.ds(start, span), :] = (mixed / total).astype(jnp.bfloat16).reshape(RATIO, span, HD)
         lse = peak * SCALE + jnp.log(total)
         stat_scr[pl.ds(start, span), :] = split_stat(lse.reshape(RATIO, span, 1), span).astype(jnp.bfloat16)
+
+    halves = (count + 15) // 16
+
+    @pl.loop(0, halves // 2)
+    def _(index):
+        work(pl.multiple_of(index * 32, 32), 32)
+
+    @pl.when(halves % 2 == 1)
+    def _():
+        work(pl.multiple_of((halves - 1) * 16, 16), 16)
 
     idle = 1.0 - valid
     mean = sum(piece[1].astype(jnp.float32).reshape(PIECE // 8, 8, HD).sum(axis=0) for piece in pieces)
@@ -381,11 +388,11 @@
     chosen = pl.pallas_call(
         select_kernel,
         out_shape=jax.ShapeDtypeStruct((KVH, 80, HD), jnp.bfloat16),
-        in_specs=[VMEM] * 2,
+        in_specs=[VMEM] * 2 + [ANY],
         out_specs=VMEM,
         compiler_params=params(8),
         name="select",
-    )(got, back)
+    )(got, back, near)
     final = lax.all_to_all(chosen, "y", 0, 0, tiled=True)
     return pl.pallas_call(
         merge_kernel,

time: 98.7 us -> 98.5 us (level)
  blocking collectives: 42.6 us -> 17.4 us
  waiting for transfers between devices: 8.46 us -> 22.7 us
  starting transfers between devices: 29.6 us -> 40.1 us
    all_to_all x1, blocking collectives: 33.6 us -> 8.41 us  [shards(): final = lax.all_to_all(chosen, 'y', 0, 0, tiled=True)]
    all_to_all x1, waiting for transfers between devices: 0.01 us -> 14.2 us  [shards(): back = lax.all_to_all(parcel, FAR, 0, 0, tiled=True)]
    all_to_all x1, starting transfers between devices: 3.29 us -> 13.8 us  [shards(): back = lax.all_to_all(parcel, FAR, 0, 0, tiled=True)]
  transfers between devices with their start and end apart: 17 -> 17, of which waited for: 7 -> 8; matrix products, arithmetic and copies ran while one was open for 0% -> 0% of each run, Pallas kernels for 7% -> 7%
where the time goes in v1:
time: 98.5 us; the launch traced here: 98.9 us
  starting transfers between devices  40.1 us (41%)
  waiting for transfers between devices  22.7 us (23%)
  blocking collectives  17.4 us (18%)
  Pallas kernels  16.7 us (17%)
  local copies, waits for them, and re-layouts  1.92 us (2%)
    all_to_all x1, waiting for transfers between devices, shards(): back = lax.all_to_all(parcel, FAR, 0, 0, tiled=True)  14.2 us
    all_to_all x1, starting transfers between devices, shards(): back = lax.all_to_all(parcel, FAR, 0, 0, tiled=True)  13.8 us
    ppermute x7, starting transfers between devices, shards(): lax.ppermute(cuts[step], NEAR, [(i, i ^ step) for i in range(8)])  13.8 us
    all_to_all x1, starting transfers between devices, shards(): lax.all_to_all(outgoing.reshape(PROMPTS, 64, HD), FAR, 0, 0, tiled=True)  10.9 us
    all_to_all x1, blocking collectives, shards(): got = lax.all_to_all(sent, 'y', 0, 0, tiled=True)  8.97 us
    all_to_all x1, blocking collectives, shards(): final = lax.all_to_all(chosen, 'y', 0, 0, tiled=True)  8.41 us
    pallas_call x1, Pallas kernels, shards(): pl.pallas_call(near_kernel, grid=(HELD,), out_shape=jax.ShapeDtypeStruct(...  7.16 us
    ppermute x7, waiting for transfers between devices, shards(): lax.ppermute(cuts[step], NEAR, [(i, i ^ step) for i in range(8)])  4.85 us
  transfers between devices with their start and end apart: 17, of which 8 were waited for; matrix products, arithmetic and copies ran while one was open for 0% of the time, Pallas kernels for 7%

profile of v1, /device:TPU:32, one launch (start us, length us, event | category | flops | bytes accessed | tf_op | source)
XLA Modules:
  0.0 98.9 jit_solution(17990221555419727396)
XLA Ops:
  0.0 2.5 %prep.1 = (bf16[4,80,128]{2,1,0:T(8,128)(2,1)}, bf16[2,256,128]{2,1,0:T(8,128)(2,1)}, bf16[2,256,128]{2,1,0:T(8,128)(2,1)}, bf16[2,256,128]{2,1,0:T(8,128)(2,1)}...) custom-call(s32[1]{0:T(128)} %bitcast.place_ref, ...), custom_call_target="tpu_custom_call" | custom-call | tf_op jit(solution)/shard_map/prep/pallas_call | solution.py:317
  2.6 1.6 %collective-permute-start = (bf16[2,256,128]{2,1,0:T(8,128)(2,1)}, bf16[2,256,128]{2,1,0:T(8,128)(2,1)S(1)}, u32[]{:S(2)}, u32[]{:S(2)}) collective-permute-start(bf16[2,256,128]{2,1,0:T(8,128)(2,1)} %get-tuple-element.15), channel_id=1, source_target_pairs={{0,8},{2,10},{4,12},{6,14},{8,0},{10,2},{12,4},{14,6},{1,9},{3,11}... | collective-permute-start | bytes 393224 | tf_op jit(solution)/shard_map/ppermute | solution.py:334
  4.2 1.5 %collective-permute-start.1 = (bf16[2,256,128]{2,1,0:T(8,128)(2,1)}, bf16[2,256,128]{2,1,0:T(8,128)(2,1)S(1)}, u32[]{:S(2)}, u32[]{:S(2)}) collective-permute-start(bf16[2,256,128]{2,1,0:T(8,128)(2,1)} %get-tuple-element.16), channel_id=1, source_target_pairs={{0,10},{2,8},{4,14},{6,12},{8,2},{10,0},{12,6},{14,4},{1,11},{3,9}... | collective-permute-start | bytes 393224 | tf_op jit(solution)/shard_map/ppermute | solution.py:334
  5.7 3.8 %collective-permute-start.2 = (bf16[2,256,128]{2,1,0:T(8,128)(2,1)}, bf16[2,256,128]{2,1,0:T(8,128)(2,1)S(1)}, u32[]{:S(2)}, u32[]{:S(2)}) collective-permute-start(bf16[2,256,128]{2,1,0:T(8,128)(2,1)} %get-tuple-element.17), channel_id=1, source_target_pairs={{0,12},{2,14},{4,8},{6,10},{8,4},{10,6},{12,0},{14,2},{1,13},{3,15... | collective-permute-start | bytes 393224 | tf_op jit(solution)/shard_map/ppermute | solution.py:334
  9.5 9.0 %all_to_all.20.got_ref = bf16[4,80,128]{2,1,0:T(8,128)(2,1)S(1)} all-to-all(bf16[4,80,128]{2,1,0:T(8,128)(2,1)} %get-tuple-element.14), channel_id=1, replica_groups=mesh['xh'=2,'z'=8,'xl'=2,'y'=4,'c'=2] {'y'}, dimensions={0} | all-to-all | bytes 163840 | tf_op jit(solution)/shard_map/all_to_all | solution.py:336
  18.5 1.5 %pack.1 = bf16[2048,128]{1,0:T(8,128)(2,1)} custom-call(bf16[4,80,128]{2,1,0:T(8,128)(2,1)S(1)} %all_to_all.20.got_ref, bf16[2,256,128]{2,1,0:T(8,128)(2,1)S(1)} %collective-permute-done.refs_0_.refs_4_, bf16[2,256,128]{2,1,0:T(8,128)(2,1)S(1)} %collective-permute-done.1.refs_1_.refs_5_, bf16[2,256,128]{2,1,0:T(8,128)(2,1)S(1)} %collective-permute-done.2.refs_2_.refs_6_), custom_call_target="tpu_custom_call" | custom-call | tf_op jit(solution)/shard_map/pack/pallas_call | solution.py:337
  20.0 10.9 %all-to-all-start.1 = ((bf16[32,64,128]{2,1,0:T(8,128)(2,1)}), bf16[32,64,128]{2,1,0:T(8,128)(2,1)S(1)}, u32[]{:S(2)}, u32[]{:S(2)}) async-start(bf16[32,64,128]{2,1,0:T(8,128)(2,1)} %bitcast.1), calls=%async_computation.1 | async-start | bytes 1048576 | tf_op jit(solution)/shard_map/all_to_all | solution.py:345
  30.9 1.3 %collective-permute-start.5 = (bf16[2,256,128]{2,1,0:T(8,128)(2,1)S(1)}, bf16[2,256,128]{2,1,0:T(8,128)(2,1)S(1)}, u32[]{:S(2)}, u32[]{:S(2)}) collective-permute-start(bf16[2,256,128]{2,1,0:T(8,128)(2,1)S(1)} %copy-done.6), channel_id=1, source_target_pairs={{0,6},{2,4},{4,2},{6,0},{8,14},{10,12},{12,10},{14,8},{1,7},{3,5},... | collective-permute-start | bytes 393224 | tf_op jit(solution)/shard_map/ppermute | solution.py:334
  32.2 3.0 %collective-permute-start.6 = (bf16[2,256,128]{2,1,0:T(8,128)(2,1)S(1)}, bf16[2,256,128]{2,1,0:T(8,128)(2,1)S(1)}, u32[]{:S(2)}, u32[]{:S(2)}) collective-permute-start(bf16[2,256,128]{2,1,0:T(8,128)(2,1)S(1)} %copy-done.5), channel_id=1, source_target_pairs={{0,14},{2,12},{4,10},{6,8},{8,6},{10,4},{12,2},{14,0},{1,15},{3,13... | collective-permute-start | bytes 393224 | tf_op jit(solution)/shard_map/ppermute | solution.py:334
  35.2 2.6 %collective-permute-start.4 = (bf16[2,256,128]{2,1,0:T(8,128)(2,1)S(1)}, bf16[2,256,128]{2,1,0:T(8,128)(2,1)S(1)}, u32[]{:S(2)}, u32[]{:S(2)}) collective-permute-start(bf16[2,256,128]{2,1,0:T(8,128)(2,1)S(1)} %copy-done.3), channel_id=1, source_target_pairs={{0,4},{2,6},{4,0},{6,2},{8,12},{10,14},{12,8},{14,10},{1,5},{3,7},... | collective-permute-start | bytes 393224 | tf_op jit(solution)/shard_map/ppermute | solution.py:334
  37.8 4.8 %collective-permute-done.5.refs_3_ = bf16[2,256,128]{2,1,0:T(8,128)(2,1)S(1)} collective-permute-done((bf16[2,256,128]{2,1,0:T(8,128)(2,1)S(1)}, bf16[2,256,128]{2,1,0:T(8,128)(2,1)S(1)}, u32[]{:S(2)}, u32[]{:S(2)}) %collective-permute-start.5) | collective-permute-done | bytes 131104 | tf_op jit(solution)/shard_map/ppermute | solution.py:334
  42.6 0.5 collective-permute-start.12
  43.1 0.1 collective-permute-start.13
  43.2 0.4 collective-permute-start.10
  43.7 0.1 collective-permute-start.14
  43.7 0.2 collective-permute-done.11.refs_12_
  44.0 0.2 collective-permute-start.8
  44.2 0.3 collective-permute-start.9
  44.5 0.2 collective-permute-done.10.refs_11_
  44.7 0.3 collective-permute-done.14.refs_15_
  45.0 0.3 collective-permute-done.8.refs_9_
  45.3 0.2 collective-permute-done.9.refs_10_
  45.5 2.3 %all-to-all-done.1 = bf16[32,64,128]{2,1,0:T(8,128)(2,1)S(1)} async-done(((bf16[32,64,128]{2,1,0:T(8,128)(2,1)}), bf16[32,64,128]{2,1,0:T(8,128)(2,1)S(1)}, u32[]{:S(2)}, u32[]{:S(2)}) %all-to-all-start.1) | async-done | bytes 524320 | tf_op jit(solution)/shard_map/all_to_all | solution.py:345
  47.9 4.3 %far.1 = bf16[32,80,128]{2,1,0:T(8,128)(2,1)} custom-call(bf16[2048,128]{1,0:T(8,128)(2,1)S(1)} %bitcast.3, bf16[2,256,128]{2,1,0:T(8,128)(2,1)S(1)} %copy-done.2, bf16[2,256,128]{2,1,0:T(8,128)(2,1)S(1)} %collective-permute-done.3.refs_1_, bf16[2,256,128]{2,1,0:T(8,128)(2,1)S(1)} %collective-permute-done.4.refs_2_, ...), custom_call_target="tpu_custom_call" | custom-call | tf_op jit(solution)/shard_map/far/pallas_call | solution.py:373
  52.1 13.8 %all-to-all-start.2 = ((bf16[32,80,128]{2,1,0:T(8,128)(2,1)}), bf16[32,80,128]{2,1,0:T(8,128)(2,1)S(1)}, u32[]{:S(2)}, u32[]{:S(2)}) async-start(bf16[32,80,128]{2,1,0:T(8,128)(2,1)} %far.1), calls=%async_computation.2 | async-start | bytes 1310720 | tf_op jit(solution)/shard_map/all_to_all | solution.py:387
  65.9 7.2 %near.1.refs_0_.near_ref = f32[64,8,128]{2,1,0:T(8,128)} custom-call(s32[8]{0:T(128)} %len_ref.1, bf16[8,4096]{1,0:T(8,128)(2,1)} %query_ref.1, bf16[8,512]{1,0:T(8,128)(2,1)} %new_key_ref.1, bf16[8,512]{1,0:T(8,128)(2,1)} %new_value_ref.1, bf16[8,256,512]{2,1,0:T(8,128)(2,1)} %key_ref.3, bf16[8,256,512]{2,1,0:T(8,128)(2,1)} %value_ref.3), custom_call_target="tpu_custom_call" | custom-call | flops 300000000 | bytes 4500000 | tf_op jit(solution)/shard_map/near/pallas_call | solution.py:347
  73.1 14.2 %all-to-all-done.2.back_ref = bf16[32,80,128]{2,1,0:T(8,128)(2,1)S(1)} async-done(((bf16[32,80,128]{2,1,0:T(8,128)(2,1)}), bf16[32,80,128]{2,1,0:T(8,128)(2,1)S(1)}, u32[]{:S(2)}, u32[]{:S(2)}) %all-to-all-start.2) | async-done | bytes 655392 | tf_op jit(solution)/shard_map/all_to_all | solution.py:387
  87.3 0.9 copy-done
  88.3 0.5 select.1
  88.8 8.4 %all_to_all.21.back_ref = bf16[4,80,128]{2,1,0:T(8,128)(2,1)S(1)} all-to-all(bf16[4,80,128]{2,1,0:T(8,128)(2,1)S(1)} %select.1), channel_id=1, replica_groups=mesh['xh'=2,'z'=8,'xl'=2,'y'=4,'c'=2] {'y'}, dimensions={0} | all-to-all | bytes 163840 | tf_op jit(solution)/shard_map/all_to_all | solution.py:396
  97.2 0.9 copy-done.1
  98.1 0.8 merge.1
  (24 shorter events, 0.1 us)
Async XLA Ops:
  2.5 28.4 %copy-start.6 = (bf16[2,256,128]{2,1,0:T(8,128)(2,1)S(1)}, bf16[2,256,128]{2,1,0:T(8,128)(2,1)}, u32[]{:S(2)}) copy-start(bf16[2,256,128]{2,1,0:T(8,128)(2,1)} %get-tuple-element.21) | copy-start | bytes 393220
  2.5 29.6 %copy-start.5 = (bf16[2,256,128]{2,1,0:T(8,128)(2,1)S(1)}, bf16[2,256,128]{2,1,0:T(8,128)(2,1)}, u32[]{:S(2)}) copy-start(bf16[2,256,128]{2,1,0:T(8,128)(2,1)} %get-tuple-element.22) | copy-start | bytes 393220
  2.6 32.6 %copy-start.4 = (bf16[2,256,128]{2,1,0:T(8,128)(2,1)S(1)}, bf16[2,256,128]{2,1,0:T(8,128)(2,1)}, u32[]{:S(2)}) copy-start(bf16[2,256,128]{2,1,0:T(8,128)(2,1)} %get-tuple-element.19) | copy-start | bytes 393220
  2.6 32.6 %copy-start.3 = (bf16[2,256,128]{2,1,0:T(8,128)(2,1)S(1)}, bf16[2,256,128]{2,1,0:T(8,128)(2,1)}, u32[]{:S(2)}) copy-start(bf16[2,256,128]{2,1,0:T(8,128)(2,1)} %get-tuple-element.20) | copy-start | bytes 393220
  2.6 35.2 %copy-start.2 = (bf16[2,256,128]{2,1,0:T(8,128)(2,1)S(1)}, bf16[2,256,128]{2,1,0:T(8,128)(2,1)}, u32[]{:S(2)}) copy-start(bf16[2,256,128]{2,1,0:T(8,128)(2,1)} %get-tuple-element.18.refs_0_) | copy-start | bytes 393220
  2.6 15.9 %collective-permute-start = (bf16[2,256,128]{2,1,0:T(8,128)(2,1)}, bf16[2,256,128]{2,1,0:T(8,128)(2,1)S(1)}, u32[]{:S(2)}, u32[]{:S(2)}) collective-permute-start(bf16[2,256,128]{2,1,0:T(8,128)(2,1)} %get-tuple-element.15), channel_id=1, source_target_pairs={{0,8},{2,10},{4,12},{6,14},{8,0},{10,2},{12,4},{14,6},{1,9},{3,11}... | collective-permute-start | bytes 393224 | tf_op jit(solution)/shard_map/ppermute | solution.py:334
  4.2 14.4 %collective-permute-start.1 = (bf16[2,256,128]{2,1,0:T(8,128)(2,1)}, bf16[2,256,128]{2,1,0:T(8,128)(2,1)S(1)}, u32[]{:S(2)}, u32[]{:S(2)}) collective-permute-start(bf16[2,256,128]{2,1,0:T(8,128)(2,1)} %get-tuple-element.16), channel_id=1, source_target_pairs={{0,10},{2,8},{4,14},{6,12},{8,2},{10,0},{12,6},{14,4},{1,11},{3,9}... | collective-permute-start | bytes 393224 | tf_op jit(solution)/shard_map/ppermute | solution.py:334
  5.7 12.8 %collective-permute-start.2 = (bf16[2,256,128]{2,1,0:T(8,128)(2,1)}, bf16[2,256,128]{2,1,0:T(8,128)(2,1)S(1)}, u32[]{:S(2)}, u32[]{:S(2)}) collective-permute-start(bf16[2,256,128]{2,1,0:T(8,128)(2,1)} %get-tuple-element.17), channel_id=1, source_target_pairs={{0,12},{2,14},{4,8},{6,10},{8,4},{10,6},{12,0},{14,2},{1,13},{3,15... | collective-permute-start | bytes 393224 | tf_op jit(solution)/shard_map/ppermute | solution.py:334
  20.0 27.9 %all-to-all-start.1 = ((bf16[32,64,128]{2,1,0:T(8,128)(2,1)}), bf16[32,64,128]{2,1,0:T(8,128)(2,1)S(1)}, u32[]{:S(2)}, u32[]{:S(2)}) async-start(bf16[32,64,128]{2,1,0:T(8,128)(2,1)} %bitcast.1), calls=%async_computation.1 | async-start | bytes 1048576 | tf_op jit(solution)/shard_map/all_to_all | solution.py:345
  30.9 11.7 %collective-permute-start.5 = (bf16[2,256,128]{2,1,0:T(8,128)(2,1)S(1)}, bf16[2,256,128]{2,1,0:T(8,128)(2,1)S(1)}, u32[]{:S(2)}, u32[]{:S(2)}) collective-permute-start(bf16[2,256,128]{2,1,0:T(8,128)(2,1)S(1)} %copy-done.6), channel_id=1, source_target_pairs={{0,6},{2,4},{4,2},{6,0},{8,14},{10,12},{12,10},{14,8},{1,7},{3,5},... | collective-permute-start | bytes 393224 | tf_op jit(solution)/shard_map/ppermute | solution.py:334
  32.2 10.4 %collective-permute-start.6 = (bf16[2,256,128]{2,1,0:T(8,128)(2,1)S(1)}, bf16[2,256,128]{2,1,0:T(8,128)(2,1)S(1)}, u32[]{:S(2)}, u32[]{:S(2)}) collective-permute-start(bf16[2,256,128]{2,1,0:T(8,128)(2,1)S(1)} %copy-done.5), channel_id=1, source_target_pairs={{0,14},{2,12},{4,10},{6,8},{8,6},{10,4},{12,2},{14,0},{1,15},{3,13... | collective-permute-start | bytes 393224 | tf_op jit(solution)/shard_map/ppermute | solution.py:334
  35.1 8.0 %collective-permute-start.3 = (bf16[2,256,128]{2,1,0:T(8,128)(2,1)S(1)}, bf16[2,256,128]{2,1,0:T(8,128)(2,1)S(1)}, u32[]{:S(2)}, u32[]{:S(2)}) collective-permute-start(bf16[2,256,128]{2,1,0:T(8,128)(2,1)S(1)} %copy-done.4), channel_id=1, source_target_pairs={{0,2},{2,0},{4,6},{6,4},{8,10},{10,8},{12,14},{14,12},{1,3},{3,1},... | collective-permute-start | bytes 393224 | tf_op jit(solution)/shard_map/ppermute | solution.py:334
  35.2 8.1 %collective-permute-start.4 = (bf16[2,256,128]{2,1,0:T(8,128)(2,1)S(1)}, bf16[2,256,128]{2,1,0:T(8,128)(2,1)S(1)}, u32[]{:S(2)}, u32[]{:S(2)}) collective-permute-start(bf16[2,256,128]{2,1,0:T(8,128)(2,1)S(1)} %copy-done.3), channel_id=1, source_target_pairs={{0,4},{2,6},{4,0},{6,2},{8,12},{10,14},{12,8},{14,10},{1,5},{3,7},... | collective-permute-start | bytes 393224 | tf_op jit(solution)/shard_map/ppermute | solution.py:334
  37.8 5.9 %collective-permute-start.7 = (bf16[2,256,128]{2,1,0:T(8,128)(2,1)S(1)}, bf16[2,256,128]{2,1,0:T(8,128)(2,1)S(1)}, u32[]{:S(2)}, u32[]{:S(2)}) collective-permute-start(bf16[2,256,128]{2,1,0:T(8,128)(2,1)S(1)} %copy-done.2), channel_id=1, source_target_pairs={{0,1},{1,0},{2,3},{3,2},{4,5},{5,4},{6,7},{7,6},{8,9},{9,8},{10,11... | collective-permute-start | bytes 393224 | tf_op jit(solution)/shard_map/ppermute | solution.py:335
  42.6 1.3 %collective-permute-start.11 = (bf16[2,256,128]{2,1,0:T(8,128)(2,1)S(1)}, bf16[2,256,128]{2,1,0:T(8,128)(2,1)S(1)}, u32[]{:S(2)}, u32[]{:S(2)}) collective-permute-start(bf16[2,256,128]{2,1,0:T(8,128)(2,1)S(1)} %collective-permute-done.refs_0_.refs_4_), channel_id=1, source_target_pairs={{0,1},{1,0},{2,3},{3,2},{4,5},{5,4},{6,7},{7,6},{8,9},{9,8},{10,11... | collective-permute-start | bytes 393224 | tf_op jit(solution)/shard_map/ppermute | solution.py:335
  42.6 1.5 %collective-permute-start.12 = (bf16[2,256,128]{2,1,0:T(8,128)(2,1)S(1)}, bf16[2,256,128]{2,1,0:T(8,128)(2,1)S(1)}, u32[]{:S(2)}, u32[]{:S(2)}) collective-permute-start(bf16[2,256,128]{2,1,0:T(8,128)(2,1)S(1)} %collective-permute-done.1.refs_1_.refs_5_), channel_id=1, source_target_pairs={{0,1},{1,0},{2,3},{3,2},{4,5},{5,4},{6,7},{7,6},{8,9},{9,8},{10,11... | collective-permute-start | bytes 393224 | tf_op jit(solution)/shard_map/ppermute | solution.py:335
  43.1 1.3 %collective-permute-start.13 = (bf16[2,256,128]{2,1,0:T(8,128)(2,1)S(1)}, bf16[2,256,128]{2,1,0:T(8,128)(2,1)S(1)}, u32[]{:S(2)}, u32[]{:S(2)}) collective-permute-start(bf16[2,256,128]{2,1,0:T(8,128)(2,1)S(1)} %collective-permute-done.2.refs_2_.refs_6_), channel_id=1, source_target_pairs={{0,1},{1,0},{2,3},{3,2},{4,5},{5,4},{6,7},{7,6},{8,9},{9,8},{10,11... | collective-permute-start | bytes 393224 | tf_op jit(solution)/shard_map/ppermute | solution.py:335
  43.2 1.4 %collective-permute-start.10 = (bf16[2,256,128]{2,1,0:T(8,128)(2,1)S(1)}, bf16[2,256,128]{2,1,0:T(8,128)(2,1)S(1)}, u32[]{:S(2)}, u32[]{:S(2)}) collective-permute-start(bf16[2,256,128]{2,1,0:T(8,128)(2,1)S(1)} %collective-permute-done.5.refs_3_), channel_id=1, source_target_pairs={{0,1},{1,0},{2,3},{3,2},{4,5},{5,4},{6,7},{7,6},{8,9},{9,8},{10,11... | collective-permute-start | bytes 393224 | tf_op jit(solution)/shard_map/ppermute | solution.py:335
  43.7 1.3 %collective-permute-start.14 = (bf16[2,256,128]{2,1,0:T(8,128)(2,1)S(1)}, bf16[2,256,128]{2,1,0:T(8,128)(2,1)S(1)}, u32[]{:S(2)}, u32[]{:S(2)}) collective-permute-start(bf16[2,256,128]{2,1,0:T(8,128)(2,1)S(1)} %collective-permute-done.6.refs_7_), channel_id=1, source_target_pairs={{0,1},{1,0},{2,3},{3,2},{4,5},{5,4},{6,7},{7,6},{8,9},{9,8},{10,11... | collective-permute-start | bytes 393224 | tf_op jit(solution)/shard_map/ppermute | solution.py:335
  44.0 1.3 %collective-permute-start.8 = (bf16[2,256,128]{2,1,0:T(8,128)(2,1)S(1)}, bf16[2,256,128]{2,1,0:T(8,128)(2,1)S(1)}, u32[]{:S(2)}, u32[]{:S(2)}) collective-permute-start(bf16[2,256,128]{2,1,0:T(8,128)(2,1)S(1)} %collective-permute-done.3.refs_1_), channel_id=1, source_target_pairs={{0,1},{1,0},{2,3},{3,2},{4,5},{5,4},{6,7},{7,6},{8,9},{9,8},{10,11... | collective-permute-start | bytes 393224 | tf_op jit(solution)/shard_map/ppermute | solution.py:335
  44.2 1.3 %collective-permute-start.9 = (bf16[2,256,128]{2,1,0:T(8,128)(2,1)S(1)}, bf16[2,256,128]{2,1,0:T(8,128)(2,1)S(1)}, u32[]{:S(2)}, u32[]{:S(2)}) collective-permute-start(bf16[2,256,128]{2,1,0:T(8,128)(2,1)S(1)} %collective-permute-done.4.refs_2_), channel_id=1, source_target_pairs={{0,1},{1,0},{2,3},{3,2},{4,5},{5,4},{6,7},{7,6},{8,9},{9,8},{10,11... | collective-permute-start | bytes 393224 | tf_op jit(solution)/shard_map/ppermute | solution.py:335
  52.1 35.2 %all-to-all-start.2 = ((bf16[32,80,128]{2,1,0:T(8,128)(2,1)}), bf16[32,80,128]{2,1,0:T(8,128)(2,1)S(1)}, u32[]{:S(2)}, u32[]{:S(2)}) async-start(bf16[32,80,128]{2,1,0:T(8,128)(2,1)} %far.1), calls=%async_computation.2 | async-start | bytes 1310720 | tf_op jit(solution)/shard_map/all_to_all | solution.py:387
  87.3 1.0 copy-start
  97.2 1.0 copy-start.1

commit v2 on v1

--- a/solution.py
+++ b/solution.py
@@ -231,16 +231,13 @@
     idle = 1.0 - valid
     mean = sum(piece[1].astype(jnp.float32).reshape(PIECE // 8, 8, HD).sum(axis=0) for piece in pieces)
     mean = jnp.sum(mean, axis=0, keepdims=True) / tokens
-    heads = []
     for h in range(RATIO):
-        spread_out = jnp.dot(gather, mixed_scr[h], preferred_element_type=jnp.float32) + idle * mean
-        heads.append(spread_out.reshape(32, 8, HD))
-    for h in range(0, RATIO, 2):
-        out_ref[:, h * 8 : h * 8 + 16] = jnp.concatenate(heads[h : h + 2], axis=1).astype(jnp.bfloat16)
+        out_ref[h] = (
+            jnp.dot(gather, mixed_scr[h], preferred_element_type=jnp.float32) + idle * mean
+        ).astype(jnp.bfloat16)
     even = split_stat(jnp.full((RATIO, SLOTS, 1), math.log(tokens), jnp.float32), SLOTS)
     stat = jnp.dot(gather, stat_scr[...], preferred_element_type=jnp.float32) + idle * even
-    stat = stat.reshape(32, 8, HD)
-    out_ref[:, 64:] = jnp.concatenate([stat, jnp.zeros_like(stat)], axis=1).astype(jnp.bfloat16)
+    out_ref[RATIO] = stat.astype(jnp.bfloat16)
 
 
 def split_stat(lse, span):
@@ -256,30 +253,23 @@
     return stat
 
 
-def select_kernel(got_ref, back_ref, *refs):
-    send_ref = refs[-1]
-    tags = [got_ref[y, 64:].astype(jnp.float32)[8:, :1].astype(jnp.int32) for y in range(KVH)]
-    lane = lax.broadcasted_iota(jnp.int32, (1, ROWS), 1)
-    lane_key = ((lane >> 1) & 3) * 512 + ((lane >> 3) & 7) * 64 + (lane >> 6) * 2 + (lane & 1)
-    tag = jnp.concatenate([tags[y] for y in range(KVH) for _ in range(RATIO)], axis=0)
-    row_key = (lax.broadcasted_iota(jnp.int32, (256, 1), 0) >> 3) * 64 + tag
-    select = (row_key == lane_key).astype(jnp.float32).astype(jnp.bfloat16)
-    far = jnp.dot(select, back_ref[:, :64].reshape(ROWS, HD), preferred_element_type=jnp.float32)
-    send_ref[:, :64] = far.astype(jnp.bfloat16).reshape(KVH, 64, HD)
-    stats = back_ref[:, 64:].astype(jnp.float32)[:, :8].reshape(SLOTS, HD).astype(jnp.bfloat16)
-    lane = lax.broadcasted_iota(jnp.int32, (1, SLOTS), 1)
-    lane_key = ((lane >> 1) & 3) * 64 + (lane >> 3) * 2 + (lane & 1)
-    row_key = (lax.broadcasted_iota(jnp.int32, (32, 1), 0) >> 3) * 64 + jnp.concatenate(tags, axis=0)
-    select = (row_key == lane_key).astype(jnp.float32).astype(jnp.bfloat16)
-    stat = jnp.dot(select, stats, preferred_element_type=jnp.float32).reshape(KVH, 8, HD)
-    send_ref[:, 64:] = jnp.concatenate([stat, jnp.zeros_like(stat)], axis=1).astype(jnp.bfloat16)
-
-
-def merge_kernel(back_ref, near_ref, out_ref):
+def merge_kernel(prompt_ref, back_ref, near_ref, out_ref):
+    slots = slots_of(prompt_ref)
+    count = HEADS * HELD
+    row = lax.broadcasted_iota(jnp.int32, (count, 1), 0)
+    slot = spread(slots, row & 7)
+    head = row >> 3
+    row_key = (head & 7) * SLOTS + (slot >> 1) * 8 + (head >> 3) * 2 + (slot & 1)
+    select = (row_key == lax.broadcasted_iota(jnp.int32, (1, ROWS), 1)).astype(jnp.float32)
+    far = jnp.dot(select.astype(jnp.bfloat16), back_ref[:ROWS, :], preferred_element_type=jnp.float32)
+    row = lax.broadcasted_iota(jnp.int32, (KVH * HELD, 1), 0)
+    slot = spread(slots, row & 7)
+    row_key = (slot >> 1) * 8 + (row >> 3) * 2 + (slot & 1)
+    select = (row_key == lax.broadcasted_iota(jnp.int32, (1, SLOTS), 1)).astype(jnp.float32)
+    stats = jnp.dot(select.astype(jnp.bfloat16), back_ref[ROWS:, :], preferred_element_type=jnp.float32)
     lane = lax.broadcasted_iota(jnp.int32, (HELD, HD), 1)
     for y in range(KVH):
-        far = back_ref[y, :64].astype(jnp.float32)
-        stat = jnp.where(lane < 24, back_ref[y, 64:].astype(jnp.float32)[:8], 0.0)
+        stat = jnp.where(lane < 24, stats[y * HELD : (y + 1) * HELD], 0.0)
         for h in range(RATIO):
             head = y * RATIO + h
             far_lse = jnp.sum(jnp.where((lane & 7) == h, stat, 0.0), axis=1, keepdims=True)
@@ -287,7 +277,7 @@
             top = jnp.maximum(far_lse, near_lse)
             far_scale = jnp.exp(far_lse - top)
             near_scale = jnp.exp(near_lse - top)
-            merged = far[h * 8 : (h + 1) * 8] * far_scale + near_ref[head] * near_scale
+            merged = far[head * HELD : (head + 1) * HELD] * far_scale + near_ref[head] * near_scale
             out_ref[:, head * HD : (head + 1) * HD] = (merged / (far_scale + near_scale)).astype(
                 jnp.bfloat16
             )
@@ -372,7 +362,7 @@
 
     parcel = pl.pallas_call(
         far_kernel,
-        out_shape=jax.ShapeDtypeStruct((PROMPTS, 80, HD), jnp.bfloat16),
+        out_shape=jax.ShapeDtypeStruct((RATIO + 1, SLOTS, HD), jnp.bfloat16),
         in_specs=[VMEM] * 17,
         out_specs=VMEM,
         scratch_shapes=[
@@ -384,24 +374,17 @@
         compiler_params=params(16),
         name="far",
     )(arrived.reshape(ROWS, HD), *held, *swapped)
-    back = lax.all_to_all(parcel, FAR, 0, 0, tiled=True)
-    chosen = pl.pallas_call(
-        select_kernel,
-        out_shape=jax.ShapeDtypeStruct((KVH, 80, HD), jnp.bfloat16),
-        in_specs=[VMEM] * 2 + [ANY],
-        out_specs=VMEM,
-        compiler_params=params(8),
-        name="select",
-    )(got, back, near)
-    final = lax.all_to_all(chosen, "y", 0, 0, tiled=True)
+    parcel = parcel.reshape(RATIO + 1, 128, CAP, HD).transpose(1, 0, 2, 3)
+    back = lax.all_to_all(parcel, FAR + ("y",), 0, 0, tiled=True)
+    back = back.transpose(1, 0, 2, 3).reshape((RATIO + 1) * SLOTS, HD)
     return pl.pallas_call(
         merge_kernel,
         out_shape=jax.ShapeDtypeStruct((HELD, HEADS * HD), jnp.bfloat16),
-        in_specs=[VMEM] * 2,
+        in_specs=[SMEM] + [VMEM] * 2,
         out_specs=VMEM,
         compiler_params=params(12),
         name="merge",
-    )(final, near)
+    )(prompt_of, back, near)
 
 
 def solution(mesh):

time: 98.5 us -> 92.8 us (0.942); the launches traced: 98.9 us -> 91.2 us
  blocking collectives: 17.4 us -> 8.97 us
    all_to_all x1 -> x0, blocking collectives: 8.41 us -> none  [shards(): final = lax.all_to_all(chosen, 'y', 0, 0, tiled=True)]
    pallas_call x2 -> x1, Pallas kernels: 4.74 us -> 3.4 us  [shards(): pl.pallas_call(far_kernel, out_shape=jax.ShapeDtypeStruct((RATIO + 1, SLO...]
    reshape x0 -> x1, local copies, waits for them, and re-layouts: none -> 1.26 us  [shards(): parcel = parcel.reshape(RATIO + 1, 128, CAP, HD).transpose(1, 0, 2, 3)]
    pallas_call x1, Pallas kernels: 0.78 us -> 1.83 us  [shards(): pl.pallas_call(merge_kernel, out_shape=jax.ShapeDtypeStruct((HELD, HEADS...]
  transfers between devices with their start and end apart: 17 -> 17, of which waited for: 8 -> 8; matrix products, arithmetic and copies ran while one was open for 0% -> 0% of each run, Pallas kernels for 7% -> 8%
where the time goes in v2:
time: 92.8 us; the launch traced here: 91.2 us
  starting transfers between devices  39.6 us (43%)
  waiting for transfers between devices  23.4 us (25%)
  Pallas kernels  16.4 us (18%)
  blocking collectives  8.97 us (10%)
  local copies, waits for them, and re-layouts  2.68 us (3%)
    all_to_all x1, waiting for transfers between devices, shards(): back = lax.all_to_all(parcel, FAR + ('y',), 0, 0, tiled=True)  14.9 us
    ppermute x7, starting transfers between devices, shards(): lax.ppermute(cuts[step], NEAR, [(i, i ^ step) for i in range(8)])  13.8 us
    all_to_all x1, starting transfers between devices, shards(): back = lax.all_to_all(parcel, FAR + ('y',), 0, 0, tiled=True)  13.3 us
    all_to_all x1, starting transfers between devices, shards(): lax.all_to_all(outgoing.reshape(PROMPTS, 64, HD), FAR, 0, 0, tiled=True)  10.9 us
    all_to_all x1, blocking collectives, shards(): got = lax.all_to_all(sent, 'y', 0, 0, tiled=True)  8.97 us
    pallas_call x1, Pallas kernels, shards(): pl.pallas_call(near_kernel, grid=(HELD,), out_shape=jax.ShapeDtypeStruct(...  7.18 us
    ppermute x7, waiting for transfers between devices, shards(): lax.ppermute(cuts[step], NEAR, [(i, i ^ step) for i in range(8)])  4.85 us
    pallas_call x1, Pallas kernels, shards(): pl.pallas_call(far_kernel, out_shape=jax.ShapeDtypeStruct((RATIO + 1, SLO...  3.4 us
  transfers between devices with their start and end apart: 17, of which 8 were waited for; matrix products, arithmetic and copies ran while one was open for 0% of the time, Pallas kernels for 8%

profile of v2, /device:TPU:32, one launch (start us, length us, event | category | flops | bytes accessed | tf_op | source)
XLA Modules:
  0.0 91.2 jit_solution(11544793675335878852)
XLA Ops:
  0.0 2.5 %prep.1 = (bf16[4,80,128]{2,1,0:T(8,128)(2,1)}, bf16[2,256,128]{2,1,0:T(8,128)(2,1)}, bf16[2,256,128]{2,1,0:T(8,128)(2,1)}, bf16[2,256,128]{2,1,0:T(8,128)(2,1)}...) custom-call(s32[1]{0:T(128)} %bitcast.place_ref, ...), custom_call_target="tpu_custom_call" | custom-call | tf_op jit(solution)/shard_map/prep/pallas_call | solution.py:307
  2.6 1.6 %collective-permute-start = (bf16[2,256,128]{2,1,0:T(8,128)(2,1)}, bf16[2,256,128]{2,1,0:T(8,128)(2,1)S(1)}, u32[]{:S(2)}, u32[]{:S(2)}) collective-permute-start(bf16[2,256,128]{2,1,0:T(8,128)(2,1)} %get-tuple-element.15), channel_id=1, source_target_pairs={{0,8},{2,10},{4,12},{6,14},{8,0},{10,2},{12,4},{14,6},{1,9},{3,11}... | collective-permute-start | bytes 393224 | tf_op jit(solution)/shard_map/ppermute | solution.py:324
  4.2 1.5 %collective-permute-start.1 = (bf16[2,256,128]{2,1,0:T(8,128)(2,1)}, bf16[2,256,128]{2,1,0:T(8,128)(2,1)S(1)}, u32[]{:S(2)}, u32[]{:S(2)}) collective-permute-start(bf16[2,256,128]{2,1,0:T(8,128)(2,1)} %get-tuple-element.16), channel_id=1, source_target_pairs={{0,10},{2,8},{4,14},{6,12},{8,2},{10,0},{12,6},{14,4},{1,11},{3,9}... | collective-permute-start | bytes 393224 | tf_op jit(solution)/shard_map/ppermute | solution.py:324
  5.7 3.8 %collective-permute-start.2 = (bf16[2,256,128]{2,1,0:T(8,128)(2,1)}, bf16[2,256,128]{2,1,0:T(8,128)(2,1)S(1)}, u32[]{:S(2)}, u32[]{:S(2)}) collective-permute-start(bf16[2,256,128]{2,1,0:T(8,128)(2,1)} %get-tuple-element.17), channel_id=1, source_target_pairs={{0,12},{2,14},{4,8},{6,10},{8,4},{10,6},{12,0},{14,2},{1,13},{3,15... | collective-permute-start | bytes 393224 | tf_op jit(solution)/shard_map/ppermute | solution.py:324
  9.5 9.0 %all_to_all.15.got_ref = bf16[4,80,128]{2,1,0:T(8,128)(2,1)S(1)} all-to-all(bf16[4,80,128]{2,1,0:T(8,128)(2,1)} %get-tuple-element.14), channel_id=1, replica_groups=mesh['xh'=2,'z'=8,'xl'=2,'y'=4,'c'=2] {'y'}, dimensions={0} | all-to-all | bytes 163840 | tf_op jit(solution)/shard_map/all_to_all | solution.py:326
  18.5 1.5 %pack.1 = bf16[2048,128]{1,0:T(8,128)(2,1)} custom-call(bf16[4,80,128]{2,1,0:T(8,128)(2,1)S(1)} %all_to_all.15.got_ref, bf16[2,256,128]{2,1,0:T(8,128)(2,1)S(1)} %collective-permute-done.refs_0_.refs_4_, bf16[2,256,128]{2,1,0:T(8,128)(2,1)S(1)} %collective-permute-done.1.refs_1_.refs_5_, bf16[2,256,128]{2,1,0:T(8,128)(2,1)S(1)} %collective-permute-done.2.refs_2_.refs_6_), custom_call_target="tpu_custom_call" | custom-call | tf_op jit(solution)/shard_map/pack/pallas_call | solution.py:327
  20.0 10.9 %all-to-all-start.1 = ((bf16[32,64,128]{2,1,0:T(8,128)(2,1)}), bf16[32,64,128]{2,1,0:T(8,128)(2,1)S(1)}, u32[]{:S(2)}, u32[]{:S(2)}) async-start(bf16[32,64,128]{2,1,0:T(8,128)(2,1)} %bitcast.1), calls=%async_computation.1 | async-start | bytes 1048576 | tf_op jit(solution)/shard_map/all_to_all | solution.py:335
  30.9 1.3 %collective-permute-start.5 = (bf16[2,256,128]{2,1,0:T(8,128)(2,1)S(1)}, bf16[2,256,128]{2,1,0:T(8,128)(2,1)S(1)}, u32[]{:S(2)}, u32[]{:S(2)}) collective-permute-start(bf16[2,256,128]{2,1,0:T(8,128)(2,1)S(1)} %copy-done.6), channel_id=1, source_target_pairs={{0,6},{2,4},{4,2},{6,0},{8,14},{10,12},{12,10},{14,8},{1,7},{3,5},... | collective-permute-start | bytes 393224 | tf_op jit(solution)/shard_map/ppermute | solution.py:324
  32.2 3.0 %collective-permute-start.6 = (bf16[2,256,128]{2,1,0:T(8,128)(2,1)S(1)}, bf16[2,256,128]{2,1,0:T(8,128)(2,1)S(1)}, u32[]{:S(2)}, u32[]{:S(2)}) collective-permute-start(bf16[2,256,128]{2,1,0:T(8,128)(2,1)S(1)} %copy-done.5), channel_id=1, source_target_pairs={{0,14},{2,12},{4,10},{6,8},{8,6},{10,4},{12,2},{14,0},{1,15},{3,13... | collective-permute-start | bytes 393224 | tf_op jit(solution)/shard_map/ppermute | solution.py:324
  35.2 2.6 %collective-permute-start.4 = (bf16[2,256,128]{2,1,0:T(8,128)(2,1)S(1)}, bf16[2,256,128]{2,1,0:T(8,128)(2,1)S(1)}, u32[]{:S(2)}, u32[]{:S(2)}) collective-permute-start(bf16[2,256,128]{2,1,0:T(8,128)(2,1)S(1)} %copy-done.3), channel_id=1, source_target_pairs={{0,4},{2,6},{4,0},{6,2},{8,12},{10,14},{12,8},{14,10},{1,5},{3,7},... | collective-permute-start | bytes 393224 | tf_op jit(solution)/shard_map/ppermute | solution.py:324
  37.8 4.8 %collective-permute-done.5.refs_3_ = bf16[2,256,128]{2,1,0:T(8,128)(2,1)S(1)} collective-permute-done((bf16[2,256,128]{2,1,0:T(8,128)(2,1)S(1)}, bf16[2,256,128]{2,1,0:T(8,128)(2,1)S(1)}, u32[]{:S(2)}, u32[]{:S(2)}) %collective-permute-start.5) | collective-permute-done | bytes 131104 | tf_op jit(solution)/shard_map/ppermute | solution.py:324
  42.6 0.5 collective-permute-start.12
  43.1 0.1 collective-permute-start.13
  43.2 0.4 collective-permute-start.10
  43.7 0.1 collective-permute-start.14
  43.7 0.2 collective-permute-done.11.refs_12_
  44.0 0.2 collective-permute-start.8
  44.2 0.3 collective-permute-start.9
  44.5 0.2 collective-permute-done.10.refs_11_
  44.7 0.3 collective-permute-done.14.refs_15_
  45.0 0.3 collective-permute-done.8.refs_9_
  45.3 0.2 collective-permute-done.9.refs_10_
  45.5 2.3 %all-to-all-done.1 = bf16[32,64,128]{2,1,0:T(8,128)(2,1)S(1)} async-done(((bf16[32,64,128]{2,1,0:T(8,128)(2,1)}), bf16[32,64,128]{2,1,0:T(8,128)(2,1)S(1)}, u32[]{:S(2)}, u32[]{:S(2)}) %all-to-all-start.1) | async-done | bytes 524320 | tf_op jit(solution)/shard_map/all_to_all | solution.py:335
  47.9 3.4 %far.1 = bf16[9,256,128]{2,1,0:T(8,128)(2,1)S(1)} custom-call(bf16[2048,128]{1,0:T(8,128)(2,1)S(1)} %bitcast.11, bf16[2,256,128]{2,1,0:T(8,128)(2,1)S(1)} %copy-done.1, bf16[2,256,128]{2,1,0:T(8,128)(2,1)S(1)} %collective-permute-done.3.refs_1_, bf16[2,256,128]{2,1,0:T(8,128)(2,1)S(1)} %collective-permute-done.4.refs_2_, ...), custom_call_target="tpu_custom_call" | custom-call | tf_op jit(solution)/shard_map/far/pallas_call | solution.py:363
  51.3 1.3 %copy.13 = bf16[9,128,2,128]{3,2,0,1:T(2,128)(2,1)} copy(bf16[9,128,2,128]{3,2,1,0:T(2,128)(2,1)S(1)} %bitcast.10) | data formatting | bytes 1179648 | tf_op jit(solution)/shard_map/reshape | solution.py:377
  52.5 13.3 %all-to-all-start.2 = ((bf16[128,9,2,128]{3,2,1,0:T(2,128)(2,1)}), bf16[128,9,2,128]{3,2,1,0:T(2,128)(2,1)S(1)}, u32[]{:S(2)}, u32[]{:S(2)}) async-start(bf16[128,9,2,128]{3,2,1,0:T(2,128)(2,1)} %bitcast.8), calls=%async_computation.2 | async-start | bytes 1179648 | tf_op jit(solution)/shard_map/all_to_all | solution.py:378
  65.8 0.0 copy-start.2
  65.9 7.2 %near.1.near_ref = f32[64,8,128]{2,1,0:T(8,128)} custom-call(s32[8]{0:T(128)} %len_ref.1, bf16[8,4096]{1,0:T(8,128)(2,1)} %query_ref.1, bf16[8,512]{1,0:T(8,128)(2,1)} %new_key_ref.1, bf16[8,512]{1,0:T(8,128)(2,1)} %new_value_ref.1, bf16[8,256,512]{2,1,0:T(8,128)(2,1)} %key_ref.3, bf16[8,256,512]{2,1,0:T(8,128)(2,1)} %value_ref.3), custom_call_target="tpu_custom_call" | custom-call | flops 300000000 | bytes 4500000 | tf_op jit(solution)/shard_map/near/pallas_call | solution.py:337
  73.0 14.9 %all-to-all-done.2 = bf16[128,9,2,128]{3,2,1,0:T(2,128)(2,1)S(1)} async-done(((bf16[128,9,2,128]{3,2,1,0:T(2,128)(2,1)}), bf16[128,9,2,128]{3,2,1,0:T(2,128)(2,1)S(1)}, u32[]{:S(2)}, u32[]{:S(2)}) %all-to-all-start.2) | async-done | bytes 589856 | tf_op jit(solution)/shard_map/all_to_all | solution.py:378
  87.9 0.5 copy.11
  88.4 0.9 %copy-done = f32[64,8,128]{2,1,0:T(8,128)S(1)} copy-done((f32[64,8,128]{2,1,0:T(8,128)S(1)}, f32[64,8,128]{2,1,0:T(8,128)}, u32[]{:S(2)}) %copy-start) | copy-done | bytes 262168
  89.4 1.8 %merge.1 = bf16[8,4096]{1,0:T(8,128)(2,1)} custom-call(s32[8]{0:T(128)S(1)} %copy-done.2, bf16[2304,128]{1,0:T(8,128)(2,1)S(1)} %bitcast.9, f32[64,8,128]{2,1,0:T(8,128)S(1)} %copy-done), custom_call_target="tpu_custom_call" | custom-call | tf_op jit(solution)/shard_map/merge/pallas_call | solution.py:380
  (24 shorter events, 0.1 us)
Async XLA Ops:
  2.5 28.4 %copy-start.6 = (bf16[2,256,128]{2,1,0:T(8,128)(2,1)S(1)}, bf16[2,256,128]{2,1,0:T(8,128)(2,1)}, u32[]{:S(2)}) copy-start(bf16[2,256,128]{2,1,0:T(8,128)(2,1)} %get-tuple-element.21) | copy-start | bytes 393220
  2.5 29.6 %copy-start.5 = (bf16[2,256,128]{2,1,0:T(8,128)(2,1)S(1)}, bf16[2,256,128]{2,1,0:T(8,128)(2,1)}, u32[]{:S(2)}) copy-start(bf16[2,256,128]{2,1,0:T(8,128)(2,1)} %get-tuple-element.22) | copy-start | bytes 393220
  2.6 32.6 %copy-start.4 = (bf16[2,256,128]{2,1,0:T(8,128)(2,1)S(1)}, bf16[2,256,128]{2,1,0:T(8,128)(2,1)}, u32[]{:S(2)}) copy-start(bf16[2,256,128]{2,1,0:T(8,128)(2,1)} %get-tuple-element.19) | copy-start | bytes 393220
  2.6 32.6 %copy-start.3 = (bf16[2,256,128]{2,1,0:T(8,128)(2,1)S(1)}, bf16[2,256,128]{2,1,0:T(8,128)(2,1)}, u32[]{:S(2)}) copy-start(bf16[2,256,128]{2,1,0:T(8,128)(2,1)} %get-tuple-element.20) | copy-start | bytes 393220
  2.6 35.2 %copy-start.1 = (bf16[2,256,128]{2,1,0:T(8,128)(2,1)S(1)}, bf16[2,256,128]{2,1,0:T(8,128)(2,1)}, u32[]{:S(2)}) copy-start(bf16[2,256,128]{2,1,0:T(8,128)(2,1)} %get-tuple-element.18.refs_0_) | copy-start | bytes 393220
  2.6 15.9 %collective-permute-start = (bf16[2,256,128]{2,1,0:T(8,128)(2,1)}, bf16[2,256,128]{2,1,0:T(8,128)(2,1)S(1)}, u32[]{:S(2)}, u32[]{:S(2)}) collective-permute-start(bf16[2,256,128]{2,1,0:T(8,128)(2,1)} %get-tuple-element.15), channel_id=1, source_target_pairs={{0,8},{2,10},{4,12},{6,14},{8,0},{10,2},{12,4},{14,6},{1,9},{3,11}... | collective-permute-start | bytes 393224 | tf_op jit(solution)/shard_map/ppermute | solution.py:324
  4.2 14.4 %collective-permute-start.1 = (bf16[2,256,128]{2,1,0:T(8,128)(2,1)}, bf16[2,256,128]{2,1,0:T(8,128)(2,1)S(1)}, u32[]{:S(2)}, u32[]{:S(2)}) collective-permute-start(bf16[2,256,128]{2,1,0:T(8,128)(2,1)} %get-tuple-element.16), channel_id=1, source_target_pairs={{0,10},{2,8},{4,14},{6,12},{8,2},{10,0},{12,6},{14,4},{1,11},{3,9}... | collective-permute-start | bytes 393224 | tf_op jit(solution)/shard_map/ppermute | solution.py:324
  5.7 12.8 %collective-permute-start.2 = (bf16[2,256,128]{2,1,0:T(8,128)(2,1)}, bf16[2,256,128]{2,1,0:T(8,128)(2,1)S(1)}, u32[]{:S(2)}, u32[]{:S(2)}) collective-permute-start(bf16[2,256,128]{2,1,0:T(8,128)(2,1)} %get-tuple-element.17), channel_id=1, source_target_pairs={{0,12},{2,14},{4,8},{6,10},{8,4},{10,6},{12,0},{14,2},{1,13},{3,15... | collective-permute-start | bytes 393224 | tf_op jit(solution)/shard_map/ppermute | solution.py:324
  20.0 27.9 %all-to-all-start.1 = ((bf16[32,64,128]{2,1,0:T(8,128)(2,1)}), bf16[32,64,128]{2,1,0:T(8,128)(2,1)S(1)}, u32[]{:S(2)}, u32[]{:S(2)}) async-start(bf16[32,64,128]{2,1,0:T(8,128)(2,1)} %bitcast.1), calls=%async_computation.1 | async-start | bytes 1048576 | tf_op jit(solution)/shard_map/all_to_all | solution.py:335
  30.9 11.7 %collective-permute-start.5 = (bf16[2,256,128]{2,1,0:T(8,128)(2,1)S(1)}, bf16[2,256,128]{2,1,0:T(8,128)(2,1)S(1)}, u32[]{:S(2)}, u32[]{:S(2)}) collective-permute-start(bf16[2,256,128]{2,1,0:T(8,128)(2,1)S(1)} %copy-done.6), channel_id=1, source_target_pairs={{0,6},{2,4},{4,2},{6,0},{8,14},{10,12},{12,10},{14,8},{1,7},{3,5},... | collective-permute-start | bytes 393224 | tf_op jit(solution)/shard_map/ppermute | solution.py:324
  32.2 10.4 %collective-permute-start.6 = (bf16[2,256,128]{2,1,0:T(8,128)(2,1)S(1)}, bf16[2,256,128]{2,1,0:T(8,128)(2,1)S(1)}, u32[]{:S(2)}, u32[]{:S(2)}) collective-permute-start(bf16[2,256,128]{2,1,0:T(8,128)(2,1)S(1)} %copy-done.5), channel_id=1, source_target_pairs={{0,14},{2,12},{4,10},{6,8},{8,6},{10,4},{12,2},{14,0},{1,15},{3,13... | collective-permute-start | bytes 393224 | tf_op jit(solution)/shard_map/ppermute | solution.py:324
  35.1 8.0 %collective-permute-start.3 = (bf16[2,256,128]{2,1,0:T(8,128)(2,1)S(1)}, bf16[2,256,128]{2,1,0:T(8,128)(2,1)S(1)}, u32[]{:S(2)}, u32[]{:S(2)}) collective-permute-start(bf16[2,256,128]{2,1,0:T(8,128)(2,1)S(1)} %copy-done.4), channel_id=1, source_target_pairs={{0,2},{2,0},{4,6},{6,4},{8,10},{10,8},{12,14},{14,12},{1,3},{3,1},... | collective-permute-start | bytes 393224 | tf_op jit(solution)/shard_map/ppermute | solution.py:324
  35.2 8.1 %collective-permute-start.4 = (bf16[2,256,128]{2,1,0:T(8,128)(2,1)S(1)}, bf16[2,256,128]{2,1,0:T(8,128)(2,1)S(1)}, u32[]{:S(2)}, u32[]{:S(2)}) collective-permute-start(bf16[2,256,128]{2,1,0:T(8,128)(2,1)S(1)} %copy-done.3), channel_id=1, source_target_pairs={{0,4},{2,6},{4,0},{6,2},{8,12},{10,14},{12,8},{14,10},{1,5},{3,7},... | collective-permute-start | bytes 393224 | tf_op jit(solution)/shard_map/ppermute | solution.py:324
  37.8 5.9 %collective-permute-start.7 = (bf16[2,256,128]{2,1,0:T(8,128)(2,1)S(1)}, bf16[2,256,128]{2,1,0:T(8,128)(2,1)S(1)}, u32[]{:S(2)}, u32[]{:S(2)}) collective-permute-start(bf16[2,256,128]{2,1,0:T(8,128)(2,1)S(1)} %copy-done.1), channel_id=1, source_target_pairs={{0,1},{1,0},{2,3},{3,2},{4,5},{5,4},{6,7},{7,6},{8,9},{9,8},{10,11... | collective-permute-start | bytes 393224 | tf_op jit(solution)/shard_map/ppermute | solution.py:325
  42.6 1.3 %collective-permute-start.11 = (bf16[2,256,128]{2,1,0:T(8,128)(2,1)S(1)}, bf16[2,256,128]{2,1,0:T(8,128)(2,1)S(1)}, u32[]{:S(2)}, u32[]{:S(2)}) collective-permute-start(bf16[2,256,128]{2,1,0:T(8,128)(2,1)S(1)} %collective-permute-done.refs_0_.refs_4_), channel_id=1, source_target_pairs={{0,1},{1,0},{2,3},{3,2},{4,5},{5,4},{6,7},{7,6},{8,9},{9,8},{10,11... | collective-permute-start | bytes 393224 | tf_op jit(solution)/shard_map/ppermute | solution.py:325
  42.6 1.5 %collective-permute-start.12 = (bf16[2,256,128]{2,1,0:T(8,128)(2,1)S(1)}, bf16[2,256,128]{2,1,0:T(8,128)(2,1)S(1)}, u32[]{:S(2)}, u32[]{:S(2)}) collective-permute-start(bf16[2,256,128]{2,1,0:T(8,128)(2,1)S(1)} %collective-permute-done.1.refs_1_.refs_5_), channel_id=1, source_target_pairs={{0,1},{1,0},{2,3},{3,2},{4,5},{5,4},{6,7},{7,6},{8,9},{9,8},{10,11... | collective-permute-start | bytes 393224 | tf_op jit(solution)/shard_map/ppermute | solution.py:325
  43.1 1.3 %collective-permute-start.13 = (bf16[2,256,128]{2,1,0:T(8,128)(2,1)S(1)}, bf16[2,256,128]{2,1,0:T(8,128)(2,1)S(1)}, u32[]{:S(2)}, u32[]{:S(2)}) collective-permute-start(bf16[2,256,128]{2,1,0:T(8,128)(2,1)S(1)} %collective-permute-done.2.refs_2_.refs_6_), channel_id=1, source_target_pairs={{0,1},{1,0},{2,3},{3,2},{4,5},{5,4},{6,7},{7,6},{8,9},{9,8},{10,11... | collective-permute-start | bytes 393224 | tf_op jit(solution)/shard_map/ppermute | solution.py:325
  43.2 1.4 %collective-permute-start.10 = (bf16[2,256,128]{2,1,0:T(8,128)(2,1)S(1)}, bf16[2,256,128]{2,1,0:T(8,128)(2,1)S(1)}, u32[]{:S(2)}, u32[]{:S(2)}) collective-permute-start(bf16[2,256,128]{2,1,0:T(8,128)(2,1)S(1)} %collective-permute-done.5.refs_3_), channel_id=1, source_target_pairs={{0,1},{1,0},{2,3},{3,2},{4,5},{5,4},{6,7},{7,6},{8,9},{9,8},{10,11... | collective-permute-start | bytes 393224 | tf_op jit(solution)/shard_map/ppermute | solution.py:325
  43.7 1.3 %collective-permute-start.14 = (bf16[2,256,128]{2,1,0:T(8,128)(2,1)S(1)}, bf16[2,256,128]{2,1,0:T(8,128)(2,1)S(1)}, u32[]{:S(2)}, u32[]{:S(2)}) collective-permute-start(bf16[2,256,128]{2,1,0:T(8,128)(2,1)S(1)} %collective-permute-done.6.refs_7_), channel_id=1, source_target_pairs={{0,1},{1,0},{2,3},{3,2},{4,5},{5,4},{6,7},{7,6},{8,9},{9,8},{10,11... | collective-permute-start | bytes 393224 | tf_op jit(solution)/shard_map/ppermute | solution.py:325
  44.0 1.3 %collective-permute-start.8 = (bf16[2,256,128]{2,1,0:T(8,128)(2,1)S(1)}, bf16[2,256,128]{2,1,0:T(8,128)(2,1)S(1)}, u32[]{:S(2)}, u32[]{:S(2)}) collective-permute-start(bf16[2,256,128]{2,1,0:T(8,128)(2,1)S(1)} %collective-permute-done.3.refs_1_), channel_id=1, source_target_pairs={{0,1},{1,0},{2,3},{3,2},{4,5},{5,4},{6,7},{7,6},{8,9},{9,8},{10,11... | collective-permute-start | bytes 393224 | tf_op jit(solution)/shard_map/ppermute | solution.py:325
  44.2 1.3 %collective-permute-start.9 = (bf16[2,256,128]{2,1,0:T(8,128)(2,1)S(1)}, bf16[2,256,128]{2,1,0:T(8,128)(2,1)S(1)}, u32[]{:S(2)}, u32[]{:S(2)}) collective-permute-start(bf16[2,256,128]{2,1,0:T(8,128)(2,1)S(1)} %collective-permute-done.4.refs_2_), channel_id=1, source_target_pairs={{0,1},{1,0},{2,3},{3,2},{4,5},{5,4},{6,7},{7,6},{8,9},{9,8},{10,11... | collective-permute-start | bytes 393224 | tf_op jit(solution)/shard_map/ppermute | solution.py:325
  52.5 35.4 %all-to-all-start.2 = ((bf16[128,9,2,128]{3,2,1,0:T(2,128)(2,1)}), bf16[128,9,2,128]{3,2,1,0:T(2,128)(2,1)S(1)}, u32[]{:S(2)}, u32[]{:S(2)}) async-start(bf16[128,9,2,128]{3,2,1,0:T(2,128)(2,1)} %bitcast.8), calls=%async_computation.2 | async-start | bytes 1179648 | tf_op jit(solution)/shard_map/all_to_all | solution.py:378
  65.8 22.6 %copy-start.2 = (s32[8]{0:T(128)S(1)}, s32[8]{0:T(128)}, u32[]{:S(2)}) copy-start(s32[8]{0:T(128)} %prompt_ref.1) | copy-start | bytes 100
  88.4 1.0 %copy-start = (f32[64,8,128]{2,1,0:T(8,128)S(1)}, f32[64,8,128]{2,1,0:T(8,128)}, u32[]{:S(2)}) copy-start(f32[64,8,128]{2,1,0:T(8,128)} %near.1.near_ref) | copy-start | bytes 786436
